TPU v7x, 512 devices: a whole 4x4x16 slice. The times are simulated.
512 devices in a mesh: seq: 32 (over x_lo, z), chan: 16 (over y, x_hi, core).
Axes of the slice: x: 4 (x_hi: 2, x_lo: 2; x = x_hi * 2 + x_lo), y: 4, z: 16, core: 2. Of those that a mesh axis runs over, the one named last changes fastest.
Arguments:
- stream_in: bfloat16 [4096, 8192], P('seq', 'chan'), may hold values from -6 to 6
- features: bfloat16 [3, 4096, 8192], P(None, 'seq', 'chan'), may hold values from -6 to 6
- conv_taps: float32 [3, 3, 8192], P(None, None, 'chan'), may hold values from -3.5 to 3.5
- decay: float32 [8192, 8], P('chan'), may hold values from 0 to 1, as said below
- residues: float32 [8192, 8], P('chan'), may hold values from -1 to 1
- state_in: float32 [8192, 8], P('chan'), may hold values from -800 to 800
- out_weight: bfloat16 [8192, 8192], P('seq', 'chan'), may hold values from -0.0625 to 0.0625
Outputs:
- block_out: bfloat16 [4096, 8192], P('seq', 'chan')
Inputs may be any that keep to these rules, and one draw needn't show every extreme that they name: `decay`: every rate is positive.
All inputs are finite; a program needn't handle non-finite values.
Results may differ from a plain program's by a relative error of at most 0.0046.
Values may be sent and summed in bfloat16 or wider, within the bound.
A program may use at most 64 MiB of HBM per device.

v0:
```python
import math

import jax
import jax.numpy as jnp
from jax import lax
from jax.sharding import PartitionSpec as P


def passed_along(block, axis, distance):
    devices = range(lax.axis_size(axis))
    route = [(i - distance, i) for i in devices if i - distance in devices]
    return lax.ppermute(block, axis, route)


def local_pass(pieces):
    mixed_in, rates, weights = pieces
    block_len = mixed_in.shape[1]
    positions = jnp.arange(block_len).astype(jnp.float32)
    offsets = (jnp.arange(block_len)[:, None] - jnp.arange(block_len)[None, :]).astype(jnp.float32)
    lower = offsets >= 0.0
    clipped = jnp.maximum(offsets, 0.0)
    toeplitz = jnp.zeros((rates.shape[0], block_len, block_len), jnp.float32)
    for pole in range(rates.shape[1]):
        term = weights[:, pole, None, None] * jnp.exp(-rates[:, pole, None, None] * clipped[None])
        toeplitz = toeplitz + jnp.where(lower[None], term, 0.0)
    inner = jnp.einsum("gij,njg->nig", toeplitz, mixed_in, precision=lax.Precision.HIGHEST)
    carried = jnp.exp(-rates[:, :, None] * (block_len - positions))
    summary = jnp.einsum("njg,grj->ngr", mixed_in, carried, precision=lax.Precision.HIGHEST)
    step_decay = jnp.exp(-rates * block_len)

    def advance(state, term):
        return (step_decay * state + term, state)

    end_state, starts = lax.scan(advance, jnp.zeros_like(rates), summary)
    return (inner, starts, end_state)


def shards(stream_in, features, conv_taps, decay, residues, state_in, out_weight):
    row_count = features.shape[1]
    chan_count = features.shape[2]
    tap_count = conv_taps.shape[1]
    pole_count = decay.shape[1]
    tails = features[:, row_count - (tap_count - 1) :, :]
    before = passed_along(tails, "seq", 1)
    joined = jnp.concatenate([before, features], axis=1).astype(jnp.float32)
    shorted = jnp.zeros((3, row_count, chan_count), jnp.float32)
    for tap in range(tap_count):
        shorted = (
            shorted
            + conv_taps[:, tap, None, :]
            * joined[:, tap_count - 1 - tap : tap_count - 1 - tap + row_count, :]
        )
    product = shorted[1] * shorted[2]
    block_len = min(128, row_count)
    block_count = row_count // block_len
    group = math.gcd(chan_count, 128)
    group_count = chan_count // group
    mixed_in = product.reshape(block_count, block_len, group_count, group).transpose(2, 0, 1, 3)
    inner, starts, end_state = lax.map(
        local_pass,
        (
            mixed_in,
            decay.reshape(group_count, group, pole_count),
            residues.reshape(group_count, group, pole_count),
        ),
    )
    inner = inner.transpose(1, 2, 0, 3).reshape(block_count, block_len, chan_count)
    starts = starts.transpose(1, 0, 2, 3).reshape(block_count, chan_count, pole_count)
    end_state = end_state.reshape(chan_count, pole_count)
    device_decay = jnp.exp(-decay * row_count)

    def relay(turn, incoming):
        return passed_along(device_decay * incoming + end_state, "seq", 1)

    prefix = lax.fori_loop(0, lax.axis_size("seq") - 1, relay, jnp.zeros_like(end_state))
    offset = lax.axis_index("seq").astype(jnp.float32) * row_count
    device_state = prefix + jnp.exp(-decay * offset) * state_in
    positions = jnp.arange(block_len).astype(jnp.float32)
    block_offsets = jnp.arange(block_count).astype(jnp.float32) * block_len
    total_starts = (
        starts + jnp.exp(-decay[None] * block_offsets[:, None, None]) * device_state[None]
    )
    outward = residues[:, :, None] * jnp.exp(-decay[:, :, None] * positions)
    cross = jnp.einsum("ngr,gri->nig", total_starts, outward, precision=lax.Precision.HIGHEST)
    filtered = (inner + cross).reshape(row_count, chan_count)
    gated = (shorted[0] * filtered).astype(jnp.bfloat16)
    whole = lax.all_gather(gated, "chan", axis=1, tiled=True)
    mixed = jnp.dot(
        whole,
        lax.all_gather(out_weight, "seq", axis=0, tiled=True),
        preferred_element_type=jnp.float32,
    )
    return (stream_in.astype(jnp.float32) + mixed).astype(jnp.bfloat16)


def solution(mesh):
    return jax.shard_map(
        shards,
        mesh=mesh,
        in_specs=(
            P("seq", "chan"),
            P(None, "seq", "chan"),
            P(None, None, "chan"),
            P("chan", None),
            P("chan", None),
            P("chan", None),
            P("seq", "chan"),
        ),
        out_specs=P("seq", "chan"),
        check_vma=False,
    )
```

profile of v0, /device:TPU:4, one launch (start us, length us, event | category | flops | bytes accessed | tf_op | source)
XLA Modules:
  0.0 564.7 jit_solution(11091360993440248402)
XLA Ops:
  21.3 70.4 %while.4 = (s32[]{:T(128)}, f32[4,1,128,128]{2,3,0,1:T(8,128)S(1)}, f32[4,1,128,8]{2,3,1,0:T(8,128)S(1)}, f32[4,128,8]{1,2,0:T(8,128)S(1)}, f32[4,1,128,128]{2,3...) while((s32[]{:T(128)}, f32[4,1,128,128]{2,3,0,1:T(8,128)S(1)}, ...), condition=%wide.region_1.2_spmd, body=%wide.region_0.1_spmd.sunk | while | flops 69686528 | bytes 971885 | solution.py:59
  22.8 14.7 %multiply_reduce_fusion.4 = f32[128,128]{1,0:T(8,128)S(1)} fusion(f32[128,128]{1,0:T(8,128)S(1)} %dynamic-slice_bitcast_fusion.6, f32[128]{0:T(128)S(1)} %get-tuple-element.230, f32[128]{0:T(128)S(1)} %get-tuple-element.231, f32[128]{0:T(128)S(1)} %get-tuple-element.232, f32[128]{0:T(128)S(1)} %get-tuple-element.233, f32[128]{0:T(128)S(1)} %get-tuple-element.234, ...), kind=kLoop, calls=%fused_computation.1.clone.1 | loop fusion | flops 69189632 | bytes 221184 | tf_op jit(solution)/shard_map/while
  40.4 14.7 %multiply_reduce_fusion.4 = f32[128,128]{1,0:T(8,128)S(1)} fusion(f32[128,128]{1,0:T(8,128)S(1)} %dynamic-slice_bitcast_fusion.6, f32[128]{0:T(128)S(1)} %get-tuple-element.230, f32[128]{0:T(128)S(1)} %get-tuple-element.231, f32[128]{0:T(128)S(1)} %get-tuple-element.232, f32[128]{0:T(128)S(1)} %get-tuple-element.233, f32[128]{0:T(128)S(1)} %get-tuple-element.234, ...), kind=kLoop, calls=%fused_computation.1.clone.1 | loop fusion | flops 69189632 | bytes 221184 | tf_op jit(solution)/shard_map/while
  58.0 14.7 %multiply_reduce_fusion.4 = f32[128,128]{1,0:T(8,128)S(1)} fusion(f32[128,128]{1,0:T(8,128)S(1)} %dynamic-slice_bitcast_fusion.6, f32[128]{0:T(128)S(1)} %get-tuple-element.230, f32[128]{0:T(128)S(1)} %get-tuple-element.231, f32[128]{0:T(128)S(1)} %get-tuple-element.232, f32[128]{0:T(128)S(1)} %get-tuple-element.233, f32[128]{0:T(128)S(1)} %get-tuple-element.234, ...), kind=kLoop, calls=%fused_computation.1.clone.1 | loop fusion | flops 69189632 | bytes 221184 | tf_op jit(solution)/shard_map/while
  75.6 14.7 %multiply_reduce_fusion.4 = f32[128,128]{1,0:T(8,128)S(1)} fusion(f32[128,128]{1,0:T(8,128)S(1)} %dynamic-slice_bitcast_fusion.6, f32[128]{0:T(128)S(1)} %get-tuple-element.230, f32[128]{0:T(128)S(1)} %get-tuple-element.231, f32[128]{0:T(128)S(1)} %get-tuple-element.232, f32[128]{0:T(128)S(1)} %get-tuple-element.233, f32[128]{0:T(128)S(1)} %get-tuple-element.234, ...), kind=kLoop, calls=%fused_computation.1.clone.1 | loop fusion | flops 69189632 | bytes 221184 | tf_op jit(solution)/shard_map/while
  91.7 208.8 %while.30 = (s32[]{:T(128)}, f32[512,8]{0,1:T(8,128)S(1)}, f32[512,8]{0,1:T(8,128)S(1)}, f32[512,8]{0,1:T(8,128)S(1)}, s32[]{:T(128)}) while((s32[]{:T(128)}, f32[512,8]{0,1:T(8,128)S(1)}, f32[512,8]{0,1:T(8,128)S(1)}, f32[512,8]{0,1:T(8,128)S(1)}, s32[]{:T(128)}) %tuple.76), condition=%wide.region_3.4_spmd, body=%wide.region_2.3_spmd.sunk | while | flops 8194 | bytes 131173 | solution.py:75
  109.0 5.5 collective-permute-start
  115.9 5.4 collective-permute-start
  122.7 5.4 collective-permute-start
  129.6 5.4 collective-permute-start
  136.4 5.4 collective-permute-start
  143.2 5.4 collective-permute-start
  150.1 5.4 collective-permute-start
  156.9 5.4 collective-permute-start
  163.7 5.4 collective-permute-start
  170.6 5.4 collective-permute-start
  177.4 5.4 collective-permute-start
  184.3 5.4 collective-permute-start
  191.1 5.4 collective-permute-start
  197.9 5.4 collective-permute-start
  286.8 5.4 collective-permute-start
  307.9 91.0 %all-gather.6.cloned.1.call-done = bf16[1,128,8192]{1,2,0:T(8,128)(2,1)} async-done(((bf16[1,128,512]{1,2,0:T(8,128)(2,1)}), bf16[1,128,8192]{1,2,0:T(8,128)(2,1)}) %all-gather.6.cloned.1.call-update) | async-done | bytes 2097168 | tf_op jit(solution)/shard_map/all_gather | solution.py:87
  398.9 152.9 %all-gather.4.cloned.1.call-done = bf16[8192,512]{1,0:T(8,128)(2,1)} async-done(((bf16[256,512]{1,0:T(8,128)(2,1)}), bf16[8192,512]{1,0:T(8,128)(2,1)}) %all-gather.4.cloned.1.call-update) | async-done | bytes 8388624 | tf_op jit(solution)/shard_map/all_gather | solution.py:90
  551.9 6.0 %fusion.10 = bf16[128,512]{1,0:T(8,128)(2,1)} fusion(bf16[8192,512]{1,0:T(8,128)(2,1)} %all-gather.4.cloned.1.call-done, bf16[1,128,8192]{1,2,0:T(8,128)(2,1)} %all-gather.6.cloned.1.call-done, bf16[128,512]{1,0:T(8,128)(2,1)S(1)} %copy-done), kind=kOutput, calls=%fused_computation.37 | convolution fusion | flops 1073938432 | bytes 10747904 | tf_op jit(solution)/shard_map/dot_general | solution.py:88
  (169 shorter events, 160.8 us)
Async XLA Ops:
  6.5 392.4 %all-gather.6.cloned.1.call-start = ((), (), s32[]{:S(2)}) async-start(), calls=%async_computation.1 | async-start | bytes 2228224 | tf_op jit(solution)/shard_map/all_gather | solution.py:87
  7.6 12.2 %collective-permute-start.1 = (bf16[3,2,512]{1,2,0:T(8,128)(2,1)S(1)}, bf16[3,2,512]{1,2,0:T(8,128)(2,1)S(1)}, u32[]{:S(2)}, u32[]{:S(2)}) collective-permute-start(bf16[3,2,512]{1,2,0:T(8,128)(2,1)S(1)} %copy.12), channel_id=1, source_target_pairs={{0,16},{16,32},{32,48},{48,64},{64,80},{80,96},{96,112},{112,128},... | collective-permute-start | bytes 18440 | tf_op jit(solution)/shard_map/ppermute | solution.py:12
  109.0 6.9 %collective-permute-start = (f32[512,8]{0,1:T(8,128)S(1)}, f32[512,8]{0,1:T(8,128)S(1)}, u32[]{:S(2)}, u32[]{:S(2)}) collective-permute-start(f32[512,8]{0,1:T(8,128)S(1)} %multiply_add_fusion.2), channel_id=1, source_target_pairs={{0,16},{16,32},{32,48},{48,64},{64,80},{80,96},{96,112},{112,128},... | collective-permute-start | bytes 49160 | tf_op jit(solution)/shard_map/while/body/eval_jaxpr/ppermute | solution.py:12
  115.9 6.8 %collective-permute-start = (f32[512,8]{0,1:T(8,128)S(1)}, f32[512,8]{0,1:T(8,128)S(1)}, u32[]{:S(2)}, u32[]{:S(2)}) collective-permute-start(f32[512,8]{0,1:T(8,128)S(1)} %multiply_add_fusion.2), channel_id=1, source_target_pairs={{0,16},{16,32},{32,48},{48,64},{64,80},{80,96},{96,112},{112,128},... | collective-permute-start | bytes 49160 | tf_op jit(solution)/shard_map/while/body/eval_jaxpr/ppermute | solution.py:12
  122.7 6.8 %collective-permute-start = (f32[512,8]{0,1:T(8,128)S(1)}, f32[512,8]{0,1:T(8,128)S(1)}, u32[]{:S(2)}, u32[]{:S(2)}) collective-permute-start(f32[512,8]{0,1:T(8,128)S(1)} %multiply_add_fusion.2), channel_id=1, source_target_pairs={{0,16},{16,32},{32,48},{48,64},{64,80},{80,96},{96,112},{112,128},... | collective-permute-start | bytes 49160 | tf_op jit(solution)/shard_map/while/body/eval_jaxpr/ppermute | solution.py:12
  129.6 6.8 %collective-permute-start = (f32[512,8]{0,1:T(8,128)S(1)}, f32[512,8]{0,1:T(8,128)S(1)}, u32[]{:S(2)}, u32[]{:S(2)}) collective-permute-start(f32[512,8]{0,1:T(8,128)S(1)} %multiply_add_fusion.2), channel_id=1, source_target_pairs={{0,16},{16,32},{32,48},{48,64},{64,80},{80,96},{96,112},{112,128},... | collective-permute-start | bytes 49160 | tf_op jit(solution)/shard_map/while/body/eval_jaxpr/ppermute | solution.py:12
  136.4 6.8 %collective-permute-start = (f32[512,8]{0,1:T(8,128)S(1)}, f32[512,8]{0,1:T(8,128)S(1)}, u32[]{:S(2)}, u32[]{:S(2)}) collective-permute-start(f32[512,8]{0,1:T(8,128)S(1)} %multiply_add_fusion.2), channel_id=1, source_target_pairs={{0,16},{16,32},{32,48},{48,64},{64,80},{80,96},{96,112},{112,128},... | collective-permute-start | bytes 49160 | tf_op jit(solution)/shard_map/while/body/eval_jaxpr/ppermute | solution.py:12
  143.2 6.8 %collective-permute-start = (f32[512,8]{0,1:T(8,128)S(1)}, f32[512,8]{0,1:T(8,128)S(1)}, u32[]{:S(2)}, u32[]{:S(2)}) collective-permute-start(f32[512,8]{0,1:T(8,128)S(1)} %multiply_add_fusion.2), channel_id=1, source_target_pairs={{0,16},{16,32},{32,48},{48,64},{64,80},{80,96},{96,112},{112,128},... | collective-permute-start | bytes 49160 | tf_op jit(solution)/shard_map/while/body/eval_jaxpr/ppermute | solution.py:12
  150.1 6.8 %collective-permute-start = (f32[512,8]{0,1:T(8,128)S(1)}, f32[512,8]{0,1:T(8,128)S(1)}, u32[]{:S(2)}, u32[]{:S(2)}) collective-permute-start(f32[512,8]{0,1:T(8,128)S(1)} %multiply_add_fusion.2), channel_id=1, source_target_pairs={{0,16},{16,32},{32,48},{48,64},{64,80},{80,96},{96,112},{112,128},... | collective-permute-start | bytes 49160 | tf_op jit(solution)/shard_map/while/body/eval_jaxpr/ppermute | solution.py:12
  156.9 6.8 %collective-permute-start = (f32[512,8]{0,1:T(8,128)S(1)}, f32[512,8]{0,1:T(8,128)S(1)}, u32[]{:S(2)}, u32[]{:S(2)}) collective-permute-start(f32[512,8]{0,1:T(8,128)S(1)} %multiply_add_fusion.2), channel_id=1, source_target_pairs={{0,16},{16,32},{32,48},{48,64},{64,80},{80,96},{96,112},{112,128},... | collective-permute-start | bytes 49160 | tf_op jit(solution)/shard_map/while/body/eval_jaxpr/ppermute | solution.py:12
  170.6 6.8 %collective-permute-start = (f32[512,8]{0,1:T(8,128)S(1)}, f32[512,8]{0,1:T(8,128)S(1)}, u32[]{:S(2)}, u32[]{:S(2)}) collective-permute-start(f32[512,8]{0,1:T(8,128)S(1)} %multiply_add_fusion.2), channel_id=1, source_target_pairs={{0,16},{16,32},{32,48},{48,64},{64,80},{80,96},{96,112},{112,128},... | collective-permute-start | bytes 49160 | tf_op jit(solution)/shard_map/while/body/eval_jaxpr/ppermute | solution.py:12
  177.4 6.8 %collective-permute-start = (f32[512,8]{0,1:T(8,128)S(1)}, f32[512,8]{0,1:T(8,128)S(1)}, u32[]{:S(2)}, u32[]{:S(2)}) collective-permute-start(f32[512,8]{0,1:T(8,128)S(1)} %multiply_add_fusion.2), channel_id=1, source_target_pairs={{0,16},{16,32},{32,48},{48,64},{64,80},{80,96},{96,112},{112,128},... | collective-permute-start | bytes 49160 | tf_op jit(solution)/shard_map/while/body/eval_jaxpr/ppermute | solution.py:12
  184.3 6.8 %collective-permute-start = (f32[512,8]{0,1:T(8,128)S(1)}, f32[512,8]{0,1:T(8,128)S(1)}, u32[]{:S(2)}, u32[]{:S(2)}) collective-permute-start(f32[512,8]{0,1:T(8,128)S(1)} %multiply_add_fusion.2), channel_id=1, source_target_pairs={{0,16},{16,32},{32,48},{48,64},{64,80},{80,96},{96,112},{112,128},... | collective-permute-start | bytes 49160 | tf_op jit(solution)/shard_map/while/body/eval_jaxpr/ppermute | solution.py:12
  191.1 6.8 %collective-permute-start = (f32[512,8]{0,1:T(8,128)S(1)}, f32[512,8]{0,1:T(8,128)S(1)}, u32[]{:S(2)}, u32[]{:S(2)}) collective-permute-start(f32[512,8]{0,1:T(8,128)S(1)} %multiply_add_fusion.2), channel_id=1, source_target_pairs={{0,16},{16,32},{32,48},{48,64},{64,80},{80,96},{96,112},{112,128},... | collective-permute-start | bytes 49160 | tf_op jit(solution)/shard_map/while/body/eval_jaxpr/ppermute | solution.py:12
  197.9 6.8 %collective-permute-start = (f32[512,8]{0,1:T(8,128)S(1)}, f32[512,8]{0,1:T(8,128)S(1)}, u32[]{:S(2)}, u32[]{:S(2)}) collective-permute-start(f32[512,8]{0,1:T(8,128)S(1)} %multiply_add_fusion.2), channel_id=1, source_target_pairs={{0,16},{16,32},{32,48},{48,64},{64,80},{80,96},{96,112},{112,128},... | collective-permute-start | bytes 49160 | tf_op jit(solution)/shard_map/while/body/eval_jaxpr/ppermute | solution.py:12
  204.8 6.8 %collective-permute-start = (f32[512,8]{0,1:T(8,128)S(1)}, f32[512,8]{0,1:T(8,128)S(1)}, u32[]{:S(2)}, u32[]{:S(2)}) collective-permute-start(f32[512,8]{0,1:T(8,128)S(1)} %multiply_add_fusion.2), channel_id=1, source_target_pairs={{0,16},{16,32},{32,48},{48,64},{64,80},{80,96},{96,112},{112,128},... | collective-permute-start | bytes 49160 | tf_op jit(solution)/shard_map/while/body/eval_jaxpr/ppermute | solution.py:12
  211.6 6.8 %collective-permute-start = (f32[512,8]{0,1:T(8,128)S(1)}, f32[512,8]{0,1:T(8,128)S(1)}, u32[]{:S(2)}, u32[]{:S(2)}) collective-permute-start(f32[512,8]{0,1:T(8,128)S(1)} %multiply_add_fusion.2), channel_id=1, source_target_pairs={{0,16},{16,32},{32,48},{48,64},{64,80},{80,96},{96,112},{112,128},... | collective-permute-start | bytes 49160 | tf_op jit(solution)/shard_map/while/body/eval_jaxpr/ppermute | solution.py:12
  218.5 6.8 %collective-permute-start = (f32[512,8]{0,1:T(8,128)S(1)}, f32[512,8]{0,1:T(8,128)S(1)}, u32[]{:S(2)}, u32[]{:S(2)}) collective-permute-start(f32[512,8]{0,1:T(8,128)S(1)} %multiply_add_fusion.2), channel_id=1, source_target_pairs={{0,16},{16,32},{32,48},{48,64},{64,80},{80,96},{96,112},{112,128},... | collective-permute-start | bytes 49160 | tf_op jit(solution)/shard_map/while/body/eval_jaxpr/ppermute | solution.py:12
  225.3 6.8 %collective-permute-start = (f32[512,8]{0,1:T(8,128)S(1)}, f32[512,8]{0,1:T(8,128)S(1)}, u32[]{:S(2)}, u32[]{:S(2)}) collective-permute-start(f32[512,8]{0,1:T(8,128)S(1)} %multiply_add_fusion.2), channel_id=1, source_target_pairs={{0,16},{16,32},{32,48},{48,64},{64,80},{80,96},{96,112},{112,128},... | collective-permute-start | bytes 49160 | tf_op jit(solution)/shard_map/while/body/eval_jaxpr/ppermute | solution.py:12
  232.1 6.8 %collective-permute-start = (f32[512,8]{0,1:T(8,128)S(1)}, f32[512,8]{0,1:T(8,128)S(1)}, u32[]{:S(2)}, u32[]{:S(2)}) collective-permute-start(f32[512,8]{0,1:T(8,128)S(1)} %multiply_add_fusion.2), channel_id=1, source_target_pairs={{0,16},{16,32},{32,48},{48,64},{64,80},{80,96},{96,112},{112,128},... | collective-permute-start | bytes 49160 | tf_op jit(solution)/shard_map/while/body/eval_jaxpr/ppermute | solution.py:12
  239.0 6.8 %collective-permute-start = (f32[512,8]{0,1:T(8,128)S(1)}, f32[512,8]{0,1:T(8,128)S(1)}, u32[]{:S(2)}, u32[]{:S(2)}) collective-permute-start(f32[512,8]{0,1:T(8,128)S(1)} %multiply_add_fusion.2), channel_id=1, source_target_pairs={{0,16},{16,32},{32,48},{48,64},{64,80},{80,96},{96,112},{112,128},... | collective-permute-start | bytes 49160 | tf_op jit(solution)/shard_map/while/body/eval_jaxpr/ppermute | solution.py:12
  245.8 6.8 %collective-permute-start = (f32[512,8]{0,1:T(8,128)S(1)}, f32[512,8]{0,1:T(8,128)S(1)}, u32[]{:S(2)}, u32[]{:S(2)}) collective-permute-start(f32[512,8]{0,1:T(8,128)S(1)} %multiply_add_fusion.2), channel_id=1, source_target_pairs={{0,16},{16,32},{32,48},{48,64},{64,80},{80,96},{96,112},{112,128},... | collective-permute-start | bytes 49160 | tf_op jit(solution)/shard_map/while/body/eval_jaxpr/ppermute | solution.py:12
  252.6 6.8 %collective-permute-start = (f32[512,8]{0,1:T(8,128)S(1)}, f32[512,8]{0,1:T(8,128)S(1)}, u32[]{:S(2)}, u32[]{:S(2)}) collective-permute-start(f32[512,8]{0,1:T(8,128)S(1)} %multiply_add_fusion.2), channel_id=1, source_target_pairs={{0,16},{16,32},{32,48},{48,64},{64,80},{80,96},{96,112},{112,128},... | collective-permute-start | bytes 49160 | tf_op jit(solution)/shard_map/while/body/eval_jaxpr/ppermute | solution.py:12
  307.1 244.7 %all-gather.4.cloned.1.call-start = ((), (), s32[]{:S(2)}) async-start(), calls=%async_computation | async-start | bytes 8650752 | tf_op jit(solution)/shard_map/all_gather | solution.py:90
  (12 other events, 804.4 us)
Sparse Core Ops, SparseCore 0:
  307.3 91.6 all-gather.5
  401.0 150.8 all-gather.3
where the time goes:
time: 567 us; the launch traced here: 565 us
  waiting for transfers between devices  293 us (52%)
  starting transfers between devices  168 us (30%)
  other arithmetic  69.8 us (12%)
  between operations  13.6 us (2%)
  matrix products  10.9 us (2%)
  local copies, waits for them, and re-layouts  8.39 us (1%)
    ppermute x32, starting transfers between devices, passed_along(): return lax.ppermute(block, axis, route)  168 us
    all_gather x1, waiting for transfers between devices, shards(): lax.all_gather(out_weight, 'seq', axis=0, tiled=True)  153 us
    all_gather x1, waiting for transfers between devices, shards(): whole = lax.all_gather(gated, 'chan', axis=1, tiled=True)  91 us
    while x8, other arithmetic  60.1 us
    ppermute x32, waiting for transfers between devices, passed_along(): return lax.ppermute(block, axis, route)  48.7 us
  transfers between devices with their start and end apart: 34, of which 34 were waited for; matrix products, arithmetic and copies ran while one was open for 1% of the time, Pallas kernels for 0%

commit v1 on v0

v1 whole, which is shorter than its diff:
```python
import jax
import jax.numpy as jnp
from jax import lax
from jax.experimental import pallas as pl
from jax.experimental.pallas import tpu as pltpu
from jax.sharding import PartitionSpec as P

MESH = pl.DeviceIdType.MESH
F32 = jnp.float32
LANES = 128
Q = 4
POLES = 8
T = 128
SUB = 8
STEPS = T // SUB
NZ = 16
NS = 32
ROUNDS = 5


def place():
    s = lax.axis_index("seq")
    c = lax.axis_index("chan")
    return s, c, s // NZ, s % NZ, c // 4, (c // 2) % 2, c % 2


def kernel(feat, taps, dec, res, sin, stream, w, out,
           wbuf, gall, gown, fraw, fpad, tail, halo, pbuf, qbuf, ybuf, xs, gf, ibuf, rbuf, sbuf, acc, cbuf,
           ws, wr, gs, gr, fs, ks, kr, hs, cs, cr, ls):
    s, c, xlo, z, y, xhi, core = place()

    def dev(xl, zz, yy, xh, co):
        return {"seq": xl * NZ + zz, "chan": yy * 4 + xh * 2 + co}

    def remote(src, dst, ssem, rsem, to):
        return pltpu.make_async_remote_copy(
            src_ref=src, dst_ref=dst, send_sem=ssem, recv_sem=rsem, device_id=to, device_id_type=MESH)

    sibling = dev(xlo, z, y, xhi, 1 - core)
    partner = dev(1 - xlo, z, y, xhi, core)
    up = dev(xlo, (z + 1) % NZ, y, xhi, core)
    down = dev(xlo, (z + NZ - 1) % NZ, y, xhi, core)

    barrier = pltpu.get_barrier_semaphore()

    def greet(to):
        pl.semaphore_signal(barrier, inc=1, device_id=to, device_id_type=MESH)

    hops = (1, 31, 2, 30, 4, 28, 8, 24, 16)
    for d in hops:
        greet({"seq": (s + d) % NS, "chan": c})
    greet(up)
    greet(down)
    greet(sibling)
    mine = xlo * 8 + y * 2 + xhi

    def greet_plane(i, carry):
        o = (mine + i) % 16
        greet(dev(o // 8, z, (o // 2) % 4, o % 2, core))
        return carry

    lax.fori_loop(1, 16, greet_plane, 0)

    load_f = pltpu.make_async_copy(feat, fraw, ls.at[Q])
    load_f.start()
    own_w = [pltpu.make_async_copy(w.at[:, pl.ds(q * LANES, LANES)], wbuf.at[q, z], ls.at[q]) for q in range(Q)]
    for o in own_w:
        o.start()
    load_f.wait()
    for i in range(3):
        fpad[i, pl.ds(8, T), :] = fraw[i].astype(F32)
        tail[pl.ds(2 * i, 2), :] = fpad[i, pl.ds(8 + T - 2, 2), :]
    tail[pl.ds(6, 2), :] = jnp.zeros((2, Q * LANES), F32)
    for o in own_w:
        o.wait()

    pl.semaphore_wait(barrier, len(hops) + 3 + 15)

    send_halo = remote(tail, halo, hs.at[0], hs.at[1], {"seq": (s + 1) % NS, "chan": c})
    send_halo.start()

    def w_copy(way, j, q):
        block = (z + NZ - j) % NZ if way == 0 else (z + j) % NZ
        return remote(wbuf.at[q, block], wbuf.at[q, block], ws.at[way, j, q], wr.at[way, j, q], up if way == 0 else down)

    def w_arrived(way, j, q):
        block = (z + NZ - j - 1) % NZ if way == 0 else (z + j + 1) % NZ
        return remote(wbuf.at[q, block], wbuf.at[q, block], ws.at[way, j, q], wr.at[way, j, q], up if way == 0 else down)

    sent = []

    def w_send(way, j, q):
        copy = w_copy(way, j, q)
        copy.start()
        sent.append((way, j, q))

    for q in range(Q):
        w_send(0, 0, q)
        w_send(1, 0, q)

    forwards = [(j, q) for j in range(1, 8) for q in range(Q)]

    def forward(count):
        for _ in range(count):
            if not forwards:
                return
            j, q = forwards.pop(0)
            for way in (0, 1):
                w_arrived(way, j - 1, q).wait_recv()
                if j < 7 or (q < 2) == (way == 0):
                    w_send(way, j, q)

    send_halo.wait_recv()
    first = s > 0
    for i in range(3):
        fpad[i, pl.ds(6, 2), :] = jnp.where(first, halo[pl.ds(2 * i, 2), :], 0.0)

    def conv(q, carry):
        cols = pl.ds(pl.multiple_of(q * LANES, LANES), LANES)

        def short(i):
            total = taps[i, 0:1, cols] * fpad[i, pl.ds(8, T), cols]
            total = total + taps[i, 1:2, cols] * fpad[i, pl.ds(7, T), cols]
            return total + taps[i, 2:3, cols] * fpad[i, pl.ds(6, T), cols]

        pbuf[q] = short(1) * short(2)
        qbuf[q] = short(0)
        return carry

    lax.fori_loop(0, Q, conv, 0)

    row = lax.broadcasted_iota(jnp.int32, (SUB, LANES), 0)

    def inner(q, carry):
        cols = pl.ds(pl.multiple_of(q * LANES, LANES), LANES)
        rates = [jnp.broadcast_to(dec[r:r + 1, cols], (SUB, LANES)) for r in range(POLES)]
        step = [jnp.exp(-v) for v in rates]
        gain = [jnp.broadcast_to(res[r:r + 1, cols], (SUB, LANES)) for r in range(POLES)]
        x = [jnp.zeros((SUB, LANES), F32) for _ in range(POLES)]
        for j in range(STEPS):
            p = pbuf[q, pl.ds(j, SUB, stride=STEPS), :]
            x = [step[r] * x[r] + p for r in range(POLES)]
            ybuf[q, j] = sum(gain[r] * x[r] for r in range(POLES))
        for r in range(POLES):
            total = step[r] * x[r]
            for d in (1, 2, 4):
                moved = jnp.where(row >= d, pltpu.roll(total, d, 0), 0.0)
                total = total + jnp.exp(rates[r] * (-1.0 * STEPS * d)) * moved
            xs[q, r] = jnp.where(row >= 1, pltpu.roll(total, 1, 0), 0.0)
            ibuf[0, q, r:r + 1, :] = total[SUB - 1:SUB, :]
        return carry

    lax.fori_loop(0, Q, inner, 0)

    def decayed(q, blocks):
        return jnp.exp(dec[:, q * LANES:(q + 1) * LANES] * (-1.0 * T * blocks))

    for q in range(Q):
        sbuf[q] = jnp.exp(dec[:, q * LANES:(q + 1) * LANES] * (-1.0 * T * s.astype(F32))) * sin[:, q * LANES:(q + 1) * LANES]
    state_sends = []
    plan = (2, 3, 3, 5, 3)
    for k in range(ROUNDS):
        d = 1 << k
        copy = remote(ibuf.at[k], rbuf.at[k], ks.at[k], kr.at[k], {"seq": (s + d) % NS, "chan": c})
        copy.start()
        state_sends.append(copy)
        forward(plan[k])
        copy.wait_recv()
        for q in range(Q):
            got = jnp.where(s >= d, rbuf[k, q], 0.0)
            sbuf[q] = sbuf[q] + decayed(q, d - 1) * got
            if k < ROUNDS - 1:
                ibuf[k + 1, q] = ibuf[k, q] + decayed(q, d) * got

    def gate(q, carry):
        cols = pl.ds(pl.multiple_of(q * LANES, LANES), LANES)
        rates = [jnp.broadcast_to(dec[r:r + 1, cols], (SUB, LANES)) for r in range(POLES)]
        step = [jnp.exp(-v) for v in rates]
        back = row.astype(F32) * (-1.0 * STEPS)
        x = []
        for r in range(POLES):
            start = xs[q, r] + jnp.exp(rates[r] * back) * sbuf[q, r:r + 1, :]
            x.append(res[r:r + 1, cols] * start)
        for j in range(STEPS):
            total = ybuf[q, j] + sum(x)
            x = [step[r] * x[r] for r in range(POLES)]
            rows = pl.ds(j, SUB, stride=STEPS)
            gf[q, rows, :] = total * qbuf[q, rows, :]
        gown[q // 2, :, pl.ds(pl.multiple_of((q % 2) * LANES, LANES), LANES)] = gf[q].astype(jnp.bfloat16)
        return carry

    lax.fori_loop(0, Q, gate, 0)

    half = y // 2
    kblk = (y % 2) * 4 + xhi * 2 + core
    spot = gall.at[xlo, pl.ds(2 * kblk, 2)]

    def g_target(i):
        o = (y * 2 + xhi + i) % 8
        return o // 2, o % 2

    for i in range(8):
        yd, xd = g_target(i)
        if i == 0:
            here = half == xlo

            @pl.when(here)
            def _():
                pltpu.make_async_copy(gown, spot, gr.at[xlo, kblk]).start()

            @pl.when(jnp.logical_not(here))
            def _():
                remote(gown, spot, gs.at[0], gr.at[xlo, kblk], dev(half, z, yd, xd, core)).start()
        else:
            remote(gown, spot, gs.at[i], gr.at[xlo, kblk], dev(half, z, yd, xd, core)).start()

    forward(8)

    def g_slot(xl, yy, xh, co):
        k = yy * 4 + xh * 2 + co
        return gall.at[xl, pl.ds(2 * k, 2)], gr.at[xl, k]

    order = [(xl, yy, xh) for xl in range(2) for yy in range(2) for xh in range(2)]
    passed = []
    for n, (xl, yy, xh) in enumerate(order):
        slot, sem = g_slot(xl, yy, xh, core)
        copy = remote(slot, slot, fs.at[n], sem, sibling)
        copy.wait_recv()
        copy.start()
        passed.append(copy)
    for xl, yy, xh in order:
        slot, sem = g_slot(xl, yy, xh, 1 - core)
        remote(slot, slot, fs.at[0], sem, sibling).wait_recv()

    def add(q, block, fresh=False):
        lhs = gall[:, block].reshape(2 * T, 2 * LANES)
        part = jnp.dot(lhs, wbuf[q, block], preferred_element_type=F32)
        acc[q] = part if fresh else acc[q] + part

    done = 7 - (len(forwards) + Q - 1) // Q

    for q in range(Q):
        add(q, z, fresh=True)

    def bulk(i, carry):
        for block in ((z + i) % NZ, (z + NZ - i) % NZ):
            for q in range(Q):
                add(q, block)
        return carry

    lax.fori_loop(1, done + 1, bulk, 0)
    while forwards:
        j = forwards[0][0]
        forward(1 if len(forwards) % Q else Q)
        if not forwards or forwards[0][0] != j:
            for block in ((z + j) % NZ, (z + NZ - j) % NZ):
                for q in range(Q):
                    add(q, block)
    sums = []
    for q in (0, 2, 1, 3):
        w_arrived(0 if q < 2 else 1, 7, q).wait_recv()
        add(q, (z + 8) % NZ)
        copy = remote(acc.at[q, pl.ds(pl.multiple_of((1 - xlo) * T, T), T)], cbuf.at[q], cs.at[q], cr.at[q], partner)
        copy.start()
        sums.append((q, copy))
    for q, copy in sums:
        copy.wait_recv()
        cols = pl.ds(q * LANES, LANES)
        mixed = acc[q, pl.ds(pl.multiple_of(xlo * T, T), T), :] + cbuf[q]
        out[:, cols] = (stream[:, cols].astype(F32) + mixed).astype(jnp.bfloat16)

    for _, copy in sums:
        copy.wait_send()
    for copy in passed:
        copy.wait_send()
    for copy in state_sends:
        copy.wait_send()
    send_halo.wait_send()
    for way, j, q in sent:
        w_copy(way, j, q).wait_send()
    for i in range(1, 8):
        remote(gown, spot, gs.at[i], gr.at[xlo, kblk], sibling).wait_send()

    @pl.when(half != xlo)
    def _():
        remote(gown, spot, gs.at[0], gr.at[xlo, kblk], sibling).wait_send()


def shards(stream_in, features, conv_taps, decay, residues, state_in, out_weight):
    vmem = pl.BlockSpec(memory_space=pltpu.VMEM)
    hbm = pl.BlockSpec(memory_space=pl.ANY)
    D = Q * LANES
    dma = pltpu.SemaphoreType.DMA
    return pl.pallas_call(
        kernel,
        out_shape=jax.ShapeDtypeStruct((T, D), jnp.bfloat16),
        in_specs=[hbm, vmem, vmem, vmem, vmem, vmem, hbm],
        out_specs=vmem,
        scratch_shapes=[
            pltpu.VMEM((Q, NZ, 2 * LANES, LANES), jnp.bfloat16),
            pltpu.VMEM((2, NZ, T, 2 * LANES), jnp.bfloat16),
            pltpu.VMEM((2, T, 2 * LANES), jnp.bfloat16),
            pltpu.VMEM((3, T, D), jnp.bfloat16),
            pltpu.VMEM((3, T + 8, D), F32),
            pltpu.VMEM((8, D), F32),
            pltpu.VMEM((8, D), F32),
            pltpu.VMEM((Q, T, LANES), F32),
            pltpu.VMEM((Q, T, LANES), F32),
            pltpu.VMEM((Q, STEPS, SUB, LANES), F32),
            pltpu.VMEM((Q, POLES, SUB, LANES), F32),
            pltpu.VMEM((Q, T, LANES), F32),
            pltpu.VMEM((ROUNDS, Q, POLES, LANES), F32),
            pltpu.VMEM((ROUNDS, Q, POLES, LANES), F32),
            pltpu.VMEM((Q, POLES, LANES), F32),
            pltpu.VMEM((Q, 2 * T, LANES), F32),
            pltpu.VMEM((Q, T, LANES), F32),
            dma((2, 8, Q)), dma((2, 8, Q)),
            dma((8,)), dma((2, 8)), dma((8,)),
            dma((ROUNDS,)), dma((ROUNDS,)),
            dma((2,)), dma((Q,)), dma((Q,)), dma((Q + 1,)),
        ],
        compiler_params=pltpu.CompilerParams(
            collective_id=0, has_side_effects=True, vmem_limit_bytes=48 * 2**20),
    )(features, conv_taps, decay.T, residues.T, state_in.T, stream_in, out_weight)


def solution(mesh):
    return jax.shard_map(
        shards,
        mesh=mesh,
        in_specs=(
            P("seq", "chan"),
            P(None, "seq", "chan"),
            P(None, None, "chan"),
            P("chan", None),
            P("chan", None),
            P("chan", None),
            P("seq", "chan"),
        ),
        out_specs=P("seq", "chan"),
        check_vma=False,
    )
```

time: 567 us -> 92.9 us (0.16)
  the two profiles are of different devices: /device:TPU:4 before, /device:TPU:1 now
where the time goes in v1:
time: 92.9 us; the launch traced here: 92.4 us
  Pallas kernels  86 us (93%)
  local copies, waits for them, and re-layouts  6.39 us (7%)
    pallas_call x1, Pallas kernels, shards(): pl.pallas_call(kernel, out_shape=jax.ShapeDtypeStruct((T, D), jnp.bfloat1...  86 us
    unnamed x15, local copies, waits for them, and re-layouts  6.39 us

profile of v1, /device:TPU:1, one launch (start us, length us, event | category | flops | bytes accessed | tf_op | source)
XLA Modules:
  0.0 92.4 jit_solution(1220921191795435138)
XLA Ops:
  0.0 0.0 copy-start
  0.0 1.0 %copy-done = bf16[3,128,512]{2,1,0:T(8,128)(2,1)S(1)} copy-done((bf16[3,128,512]{2,1,0:T(8,128)(2,1)S(1)}, bf16[3,128,512]{2,1,0:T(8,128)(2,1)}, u32[]{:S(2)}) %copy-start) | copy-done | bytes 393240
  1.0 0.0 copy-start.1
  1.0 0.9 %copy-done.1 = bf16[256,512]{1,0:T(8,128)(2,1)S(1)} copy-done((bf16[256,512]{1,0:T(8,128)(2,1)S(1)}, bf16[256,512]{1,0:T(8,128)(2,1)}, u32[]{:S(2)}) %copy-start.1) | copy-done | bytes 262168
  1.9 0.0 copy-start.2
  1.9 0.9 copy-done.2
  2.9 0.0 copy-start.3
  2.9 0.7 copy-done.3
  3.6 0.0 copy-start.4
  3.6 0.7 copy-done.4
  4.3 0.0 copy-start.5
  4.3 0.7 copy-done.5
  5.0 0.0 copy-start.6
  5.0 0.7 copy-done.6
  5.7 86.0 %shard_map.73 = bf16[128,512]{1,0:T(8,128)(2,1)S(1)} custom-call(bf16[3,128,512]{2,1,0:T(8,128)(2,1)S(1)} %copy-done, f32[3,3,512]{2,1,0:T(4,128)S(1)} %copy-done.3, f32[8,512]{1,0:T(8,128)S(1)} %bitcast.3, f32[8,512]{1,0:T(8,128)S(1)} %bitcast.4, f32[8,512]{1,0:T(8,128)S(1)} %bitcast.5, bf16[128,512]{1,0:T(8,128)(2,1)S(1)} %copy-done.2, ...), custom_call_target="tpu_custom_call" | custom-call | tf_op jit(solution)/shard_map/pallas_call | solution.py:294
  91.8 0.7 copy.9
Async XLA Ops:
  0.0 1.0 %copy-start = (bf16[3,128,512]{2,1,0:T(8,128)(2,1)S(1)}, bf16[3,128,512]{2,1,0:T(8,128)(2,1)}, u32[]{:S(2)}) copy-start(bf16[3,128,512]{2,1,0:T(8,128)(2,1)} %feat.1) | copy-start | bytes 1179652
  1.0 0.9 %copy-start.1 = (bf16[256,512]{1,0:T(8,128)(2,1)S(1)}, bf16[256,512]{1,0:T(8,128)(2,1)}, u32[]{:S(2)}) copy-start(bf16[256,512]{1,0:T(8,128)(2,1)} %w.1) | copy-start | bytes 786436
  1.9 0.9 copy-start.2
  2.9 0.7 copy-start.3
  3.6 0.7 copy-start.4
  4.3 0.7 copy-start.5
  5.0 0.7 copy-start.6

commit v2 on v1

--- a/solution.py
+++ b/solution.py
@@ -15,7 +15,7 @@
 STEPS = T // SUB
 NZ = 16
 NS = 32
-ROUNDS = 5
+ROUNDS = ((1, 2, 3), (4, 8, 12), (16,))
 
 
 def place():
@@ -24,9 +24,9 @@
     return s, c, s // NZ, s % NZ, c // 4, (c // 2) % 2, c % 2
 
 
-def kernel(feat, taps, dec, res, sin, stream, w, out,
-           wbuf, gall, gown, fraw, fpad, tail, halo, pbuf, qbuf, ybuf, xs, gf, ibuf, rbuf, sbuf, acc, cbuf,
-           ws, wr, gs, gr, fs, ks, kr, hs, cs, cr, ls):
+def kernel(feat, taps_h, dec_h, res_h, sin_h, stream_h, w, out,
+           taps, dec, res, sin, stream, wbuf, gall, gown, fraw, fpad, tail, halo, pbuf, qbuf, ybuf, xs, gf, ibuf, rbuf, sbuf, acc, cbuf,
+           ws, wr, gs, gr, ys, sr, fs, ks, kr, hs, cs, cr, ls):
     s, c, xlo, z, y, xhi, core = place()
 
     def dev(xl, zz, yy, xh, co):
@@ -46,7 +46,7 @@
     def greet(to):
         pl.semaphore_signal(barrier, inc=1, device_id=to, device_id_type=MESH)
 
-    hops = (1, 31, 2, 30, 4, 28, 8, 24, 16)
+    hops = (1, 31, 2, 30, 3, 29, 4, 28, 8, 24, 12, 20, 16)
     for d in hops:
         greet({"seq": (s + d) % NS, "chan": c})
     greet(up)
@@ -66,12 +66,16 @@
     own_w = [pltpu.make_async_copy(w.at[:, pl.ds(q * LANES, LANES)], wbuf.at[q, z], ls.at[q]) for q in range(Q)]
     for o in own_w:
         o.start()
+    small = [pltpu.make_async_copy(a, b, ls.at[Q + 1 + n]) for n, (a, b) in enumerate(
+        ((taps_h, taps), (dec_h, dec), (res_h, res), (sin_h, sin), (stream_h, stream)))]
+    for o in small:
+        o.start()
     load_f.wait()
     for i in range(3):
         fpad[i, pl.ds(8, T), :] = fraw[i].astype(F32)
         tail[pl.ds(2 * i, 2), :] = fpad[i, pl.ds(8 + T - 2, 2), :]
     tail[pl.ds(6, 2), :] = jnp.zeros((2, Q * LANES), F32)
-    for o in own_w:
+    for o in own_w + small:
         o.wait()
 
     pl.semaphore_wait(barrier, len(hops) + 3 + 15)
@@ -158,19 +162,24 @@
     for q in range(Q):
         sbuf[q] = jnp.exp(dec[:, q * LANES:(q + 1) * LANES] * (-1.0 * T * s.astype(F32))) * sin[:, q * LANES:(q + 1) * LANES]
     state_sends = []
-    plan = (2, 3, 3, 5, 3)
-    for k in range(ROUNDS):
-        d = 1 << k
-        copy = remote(ibuf.at[k], rbuf.at[k], ks.at[k], kr.at[k], {"seq": (s + d) % NS, "chan": c})
-        copy.start()
-        state_sends.append(copy)
+    plan = (4, 5, 3)
+    slot = 0
+    for k, distances in enumerate(ROUNDS):
+        copies = [remote(ibuf.at[k], rbuf.at[slot + n], ks.at[slot + n], kr.at[slot + n], {"seq": (s + d) % NS, "chan": c})
+                  for n, d in enumerate(distances)]
+        for copy in copies:
+            copy.start()
         forward(plan[k])
-        copy.wait_recv()
-        for q in range(Q):
-            got = jnp.where(s >= d, rbuf[k, q], 0.0)
-            sbuf[q] = sbuf[q] + decayed(q, d - 1) * got
-            if k < ROUNDS - 1:
-                ibuf[k + 1, q] = ibuf[k, q] + decayed(q, d) * got
+        for n, d in enumerate(distances):
+            copies[n].wait_recv()
+            for q in range(Q):
+                got = jnp.where(s >= d, rbuf[slot + n, q], 0.0)
+                sbuf[q] = sbuf[q] + decayed(q, d - 1) * got
+                if k < len(ROUNDS) - 1:
+                    before = ibuf[k, q] if n == 0 else ibuf[k + 1, q]
+                    ibuf[k + 1, q] = before + decayed(q, d) * got
+        slot += len(distances)
+        state_sends += copies
 
     def gate(q, carry):
         cols = pl.ds(pl.multiple_of(q * LANES, LANES), LANES)
@@ -191,49 +200,81 @@
 
     lax.fori_loop(0, Q, gate, 0)
 
-    half = y // 2
-    kblk = (y % 2) * 4 + xhi * 2 + core
-    spot = gall.at[xlo, pl.ds(2 * kblk, 2)]
-
-    def g_target(i):
-        o = (y * 2 + xhi + i) % 8
-        return o // 2, o % 2
-
-    for i in range(8):
-        yd, xd = g_target(i)
-        if i == 0:
-            here = half == xlo
-
-            @pl.when(here)
-            def _():
-                pltpu.make_async_copy(gown, spot, gr.at[xlo, kblk]).start()
-
-            @pl.when(jnp.logical_not(here))
-            def _():
-                remote(gown, spot, gs.at[0], gr.at[xlo, kblk], dev(half, z, yd, xd, core)).start()
-        else:
-            remote(gown, spot, gs.at[i], gr.at[xlo, kblk], dev(half, z, yd, xd, core)).start()
-
-    forward(8)
-
-    def g_slot(xl, yy, xh, co):
+    def spot(yy):
+        other = (yy // 2 + xlo) % 2
+        k = ((yy % 2) * 4 + xhi * 2 + core) * (1 - other) + (yy % 2) * other
+        return gall.at[xlo * (1 - other) + 2 * other, pl.ds(2 * k, 2)]
+
+    def landing(yy):
+        k = (yy % 2) * 4 + xhi * 2 + core
+        return gall.at[xlo, pl.ds(2 * k, 2)], gr.at[xlo, k]
+
+    def along_x(dx):
+        x = (xhi * 2 + xlo + dx) % 4
+        return dev(x % 2, z, y, x // 2, core)
+
+    def send_x(n, src):
+        yy = (y + n) % 4
+        dst, sem = landing(yy)
+        same = yy // 2 == xlo
+
+        @pl.when(same)
+        def _():
+            remote(src, dst, gs.at[n, 0], sem, along_x(2)).start()
+
+        @pl.when(jnp.logical_not(same))
+        def _():
+            remote(src, dst, gs.at[n, 0], sem, along_x(1)).start()
+            remote(src, dst, gs.at[n, 1], sem, along_x(3)).start()
+
+    home = y // 2 == xlo
+
+    @pl.when(home)
+    def _():
+        pltpu.make_async_copy(gown, spot(y), sr.at[y]).start()
+
+    send_x(0, gown)
+    y_sends = [remote(gown, spot(y), ys.at[n], sr.at[y], dev(xlo, z, (y + n) % 4, xhi, core)) for n in (1, 2, 3)]
+    for copy in y_sends:
+        copy.start()
+    passed = []
+
+    def to_sibling(slot, sem):
+        copy = remote(slot, slot, fs.at[len(passed)], sem, sibling)
+        copy.start()
+        passed.append((slot, sem))
+
+    forward(3)
+    for n in (1, 3, 2):
+        yy = (y + n) % 4
+        remote(spot(yy), spot(yy), ys.at[n], sr.at[yy], sibling).wait_recv()
+        send_x(n, spot(yy))
+        forward(1)
+
+    def arrived(xl, yy, xh, co):
         k = yy * 4 + xh * 2 + co
         return gall.at[xl, pl.ds(2 * k, 2)], gr.at[xl, k]
 
-    order = [(xl, yy, xh) for xl in range(2) for yy in range(2) for xh in range(2)]
-    passed = []
-    for n, (xl, yy, xh) in enumerate(order):
-        slot, sem = g_slot(xl, yy, xh, core)
-        copy = remote(slot, slot, fs.at[n], sem, sibling)
-        copy.wait_recv()
-        copy.start()
-        passed.append(copy)
-    for xl, yy, xh in order:
-        slot, sem = g_slot(xl, yy, xh, 1 - core)
-        remote(slot, slot, fs.at[0], sem, sibling).wait_recv()
+    @pl.when(home)
+    def _():
+        pltpu.make_async_copy(gown, spot(y), sr.at[y]).wait()
+
+    for yy in range(2):
+        to_sibling(*arrived(xlo, yy, xhi, core))
+    for yy in range(2):
+        for xl, xh in ((1 - xlo, xhi), (1 - xlo, 1 - xhi), (xlo, 1 - xhi)):
+            slot, sem = arrived(xl, yy, xh, core)
+            remote(slot, slot, fs.at[0], sem, sibling).wait_recv()
+            to_sibling(slot, sem)
+        forward(1)
+    for xl in range(2):
+        for yy in range(2):
+            for xh in range(2):
+                slot, sem = arrived(xl, yy, xh, 1 - core)
+                remote(slot, slot, fs.at[0], sem, sibling).wait_recv()
 
     def add(q, block, fresh=False):
-        lhs = gall[:, block].reshape(2 * T, 2 * LANES)
+        lhs = gall[pl.ds(0, 2), block].reshape(2 * T, 2 * LANES)
         part = jnp.dot(lhs, wbuf[q, block], preferred_element_type=F32)
         acc[q] = part if fresh else acc[q] + part
 
@@ -271,19 +312,22 @@
 
     for _, copy in sums:
         copy.wait_send()
-    for copy in passed:
-        copy.wait_send()
+    for n, (slot, sem) in enumerate(passed):
+        remote(slot, slot, fs.at[n], sem, sibling).wait_send()
     for copy in state_sends:
         copy.wait_send()
     send_halo.wait_send()
     for way, j, q in sent:
         w_copy(way, j, q).wait_send()
-    for i in range(1, 8):
-        remote(gown, spot, gs.at[i], gr.at[xlo, kblk], sibling).wait_send()
-
-    @pl.when(half != xlo)
-    def _():
-        remote(gown, spot, gs.at[0], gr.at[xlo, kblk], sibling).wait_send()
+    for copy in y_sends:
+        copy.wait_send()
+    for n in range(4):
+        dst, sem = landing((y + n) % 4)
+        remote(gown, dst, gs.at[n, 0], sem, sibling).wait_send()
+
+        @pl.when((y + n) % 4 // 2 != xlo)
+        def _():
+            remote(gown, dst, gs.at[n, 1], sem, sibling).wait_send()
 
 
 def shards(stream_in, features, conv_taps, decay, residues, state_in, out_weight):
@@ -294,11 +338,16 @@
     return pl.pallas_call(
         kernel,
         out_shape=jax.ShapeDtypeStruct((T, D), jnp.bfloat16),
-        in_specs=[hbm, vmem, vmem, vmem, vmem, vmem, hbm],
+        in_specs=[hbm] * 7,
         out_specs=vmem,
         scratch_shapes=[
+            pltpu.VMEM((3, 3, D), F32),
+            pltpu.VMEM((POLES, D), F32),
+            pltpu.VMEM((POLES, D), F32),
+            pltpu.VMEM((POLES, D), F32),
+            pltpu.VMEM((T, D), jnp.bfloat16),
             pltpu.VMEM((Q, NZ, 2 * LANES, LANES), jnp.bfloat16),
-            pltpu.VMEM((2, NZ, T, 2 * LANES), jnp.bfloat16),
+            pltpu.VMEM((3, NZ, T, 2 * LANES), jnp.bfloat16),
             pltpu.VMEM((2, T, 2 * LANES), jnp.bfloat16),
             pltpu.VMEM((3, T, D), jnp.bfloat16),
             pltpu.VMEM((3, T + 8, D), F32),
@@ -309,18 +358,18 @@
             pltpu.VMEM((Q, STEPS, SUB, LANES), F32),
             pltpu.VMEM((Q, POLES, SUB, LANES), F32),
             pltpu.VMEM((Q, T, LANES), F32),
-            pltpu.VMEM((ROUNDS, Q, POLES, LANES), F32),
-            pltpu.VMEM((ROUNDS, Q, POLES, LANES), F32),
+            pltpu.VMEM((len(ROUNDS), Q, POLES, LANES), F32),
+            pltpu.VMEM((7, Q, POLES, LANES), F32),
             pltpu.VMEM((Q, POLES, LANES), F32),
             pltpu.VMEM((Q, 2 * T, LANES), F32),
             pltpu.VMEM((Q, T, LANES), F32),
             dma((2, 8, Q)), dma((2, 8, Q)),
-            dma((8,)), dma((2, 8)), dma((8,)),
-            dma((ROUNDS,)), dma((ROUNDS,)),
-            dma((2,)), dma((Q,)), dma((Q,)), dma((Q + 1,)),
+            dma((4, 2)), dma((2, 8)), dma((4,)), dma((4,)), dma((8,)),
+            dma((7,)), dma((7,)),
+            dma((2,)), dma((Q,)), dma((Q,)), dma((Q + 6,)),
         ],
         compiler_params=pltpu.CompilerParams(
-            collective_id=0, has_side_effects=True, vmem_limit_bytes=48 * 2**20),
+            collective_id=0, has_side_effects=True, vmem_limit_bytes=60 * 2**20),
     )(features, conv_taps, decay.T, residues.T, state_in.T, stream_in, out_weight)
 
 

time: 92.9 us -> 81.3 us (0.88)
  the two profiles are of different devices: /device:TPU:1 before, /device:TPU:4 now
where the time goes in v2:
time: 81.3 us; the launch traced here: 80.7 us
  Pallas kernels  79.1 us (97%)
  local copies, waits for them, and re-layouts  1.57 us (2%)
    pallas_call x1, Pallas kernels, shards(): pl.pallas_call(kernel, out_shape=jax.ShapeDtypeStruct((T, D), jnp.bfloat1...  79.1 us

profile of v2, /device:TPU:4, one launch (start us, length us, event | category | flops | bytes accessed | tf_op | source)
XLA Modules:
  0.0 80.7 jit_solution(15350662335034627651)
XLA Ops:
  0.0 79.1 %shard_map.73 = bf16[128,512]{1,0:T(8,128)(2,1)} custom-call(bf16[3,128,512]{2,1,0:T(8,128)(2,1)} %feat.1, f32[3,3,512]{2,1,0:T(4,128)} %taps_h.1, f32[8,512]{1,0:T(8,128)} %bitcast.3, f32[8,512]{1,0:T(8,128)} %bitcast.4, f32[8,512]{1,0:T(8,128)} %bitcast.5, bf16[128,512]{1,0:T(8,128)(2,1)} %stream_h.1, bf16[256,512]{1,0:T(8,128)(2,1)} %w.1), custom_call_target="tpu_custom_call" | custom-call | tf_op jit(solution)/shard_map/pallas_call | solution.py:338
  79.1 1.6 %copy.9 = bf16[128,512]{1,0:T(8,128)(2,1)} copy(bf16[128,512]{1,0:T(8,128)(2,1)} %shard_map.73) | data formatting | bytes 262144

commit v3 on v2

--- a/solution.py
+++ b/solution.py
@@ -5,9 +5,17 @@
 from jax.experimental.pallas import tpu as pltpu
 from jax.sharding import PartitionSpec as P
 
+FIRST, EACH = 3.6, 1.45
+STATE_AT = (10.0, 17.0, 19.5)
+Y_AT = {1: 25.0, 3: 26.0, 2: 28.5}
+X_AT = (29.0, 30.0, 31.0, 33.0, 35.0, 36.0)
+SIBLING_AT = 37.0
+DOT = 0.25
+
 MESH = pl.DeviceIdType.MESH
 F32 = jnp.float32
 LANES = 128
+WIDE = 256
 Q = 4
 POLES = 8
 T = 128
@@ -25,7 +33,7 @@
 
 
 def kernel(feat, taps_h, dec_h, res_h, sin_h, stream_h, w, out,
-           taps, dec, res, sin, stream, wbuf, gall, gown, fraw, fpad, tail, halo, pbuf, qbuf, ybuf, xs, gf, ibuf, rbuf, sbuf, acc, cbuf,
+           taps, dec, res, sin, stream, wbuf, gall, gown, fraw, fpad, tail, halo, pbuf, qbuf, ybuf, xs, gf, ibuf, rbuf, sbuf, acc, csrc, cbuf,
            ws, wr, gs, gr, ys, sr, fs, ks, kr, hs, cs, cr, ls):
     s, c, xlo, z, y, xhi, core = place()
 
@@ -63,7 +71,7 @@
 
     load_f = pltpu.make_async_copy(feat, fraw, ls.at[Q])
     load_f.start()
-    own_w = [pltpu.make_async_copy(w.at[:, pl.ds(q * LANES, LANES)], wbuf.at[q, z], ls.at[q]) for q in range(Q)]
+    own_w = [pltpu.make_async_copy(w.at[:, pl.ds(n * WIDE, WIDE)], wbuf.at[n, z], ls.at[n]) for n in range(2)]
     for o in own_w:
         o.start()
     small = [pltpu.make_async_copy(a, b, ls.at[Q + 1 + n]) for n, (a, b) in enumerate(
@@ -83,13 +91,16 @@
     send_halo = remote(tail, halo, hs.at[0], hs.at[1], {"seq": (s + 1) % NS, "chan": c})
     send_halo.start()
 
+    def chunk(block, q):
+        return wbuf.at[q // 2, block, pl.ds(q % 2 * LANES, LANES)]
+
     def w_copy(way, j, q):
         block = (z + NZ - j) % NZ if way == 0 else (z + j) % NZ
-        return remote(wbuf.at[q, block], wbuf.at[q, block], ws.at[way, j, q], wr.at[way, j, q], up if way == 0 else down)
+        return remote(chunk(block, q), chunk(block, q), ws.at[way, j, q], wr.at[way, j, q], up if way == 0 else down)
 
     def w_arrived(way, j, q):
         block = (z + NZ - j - 1) % NZ if way == 0 else (z + j + 1) % NZ
-        return remote(wbuf.at[q, block], wbuf.at[q, block], ws.at[way, j, q], wr.at[way, j, q], up if way == 0 else down)
+        return remote(chunk(block, q), chunk(block, q), ws.at[way, j, q], wr.at[way, j, q], up if way == 0 else down)
 
     sent = []
 
@@ -104,14 +115,12 @@
 
     forwards = [(j, q) for j in range(1, 8) for q in range(Q)]
 
-    def forward(count):
-        for _ in range(count):
-            if not forwards:
-                return
+    def until(t):
+        while forwards and FIRST + EACH * (4 * (forwards[0][0] - 1) + forwards[0][1]) <= t:
             j, q = forwards.pop(0)
             for way in (0, 1):
                 w_arrived(way, j - 1, q).wait_recv()
-                if j < 7 or (q < 2) == (way == 0):
+                if j < 7 or q % 2 == way:
                     w_send(way, j, q)
 
     send_halo.wait_recv()
@@ -162,14 +171,13 @@
     for q in range(Q):
         sbuf[q] = jnp.exp(dec[:, q * LANES:(q + 1) * LANES] * (-1.0 * T * s.astype(F32))) * sin[:, q * LANES:(q + 1) * LANES]
     state_sends = []
-    plan = (4, 5, 3)
     slot = 0
     for k, distances in enumerate(ROUNDS):
         copies = [remote(ibuf.at[k], rbuf.at[slot + n], ks.at[slot + n], kr.at[slot + n], {"seq": (s + d) % NS, "chan": c})
                   for n, d in enumerate(distances)]
         for copy in copies:
             copy.start()
-        forward(plan[k])
+        until(STATE_AT[k])
         for n, d in enumerate(distances):
             copies[n].wait_recv()
             for q in range(Q):
@@ -244,12 +252,11 @@
         copy.start()
         passed.append((slot, sem))
 
-    forward(3)
     for n in (1, 3, 2):
+        until(Y_AT[n])
         yy = (y + n) % 4
         remote(spot(yy), spot(yy), ys.at[n], sr.at[yy], sibling).wait_recv()
         send_x(n, spot(yy))
-        forward(1)
 
     def arrived(xl, yy, xh, co):
         k = yy * 4 + xh * 2 + co
@@ -263,54 +270,49 @@
         to_sibling(*arrived(xlo, yy, xhi, core))
     for yy in range(2):
         for xl, xh in ((1 - xlo, xhi), (1 - xlo, 1 - xhi), (xlo, 1 - xhi)):
+            until(X_AT[len(passed) - 2])
             slot, sem = arrived(xl, yy, xh, core)
             remote(slot, slot, fs.at[0], sem, sibling).wait_recv()
             to_sibling(slot, sem)
-        forward(1)
+    until(SIBLING_AT)
     for xl in range(2):
         for yy in range(2):
             for xh in range(2):
                 slot, sem = arrived(xl, yy, xh, 1 - core)
                 remote(slot, slot, fs.at[0], sem, sibling).wait_recv()
 
-    def add(q, block, fresh=False):
-        lhs = gall[pl.ds(0, 2), block].reshape(2 * T, 2 * LANES)
-        part = jnp.dot(lhs, wbuf[q, block], preferred_element_type=F32)
-        acc[q] = part if fresh else acc[q] + part
-
-    done = 7 - (len(forwards) + Q - 1) // Q
-
-    for q in range(Q):
-        add(q, z, fresh=True)
-
-    def bulk(i, carry):
+    def add(n, block, fresh=False):
+        lhs = gall[pl.ds(0, 2), block].reshape(2 * T, WIDE)
+        part = jnp.dot(lhs, wbuf[n, block], preferred_element_type=F32)
+        acc[n] = part if fresh else acc[n] + part
+
+    clock = SIBLING_AT
+    for n in range(2):
+        add(n, z, fresh=True)
+    for i in range(1, 8):
         for block in ((z + i) % NZ, (z + NZ - i) % NZ):
-            for q in range(Q):
-                add(q, block)
-        return carry
-
-    lax.fori_loop(1, done + 1, bulk, 0)
-    while forwards:
-        j = forwards[0][0]
-        forward(1 if len(forwards) % Q else Q)
-        if not forwards or forwards[0][0] != j:
-            for block in ((z + j) % NZ, (z + NZ - j) % NZ):
-                for q in range(Q):
-                    add(q, block)
+            clock += DOT
+            until(clock)
+            while forwards and forwards[0][0] <= i:
+                until(FIRST + EACH * (4 * (forwards[0][0] - 1) + forwards[0][1]))
+            for n in range(2):
+                add(n, block)
     sums = []
-    for q in (0, 2, 1, 3):
-        w_arrived(0 if q < 2 else 1, 7, q).wait_recv()
-        add(q, (z + 8) % NZ)
-        copy = remote(acc.at[q, pl.ds(pl.multiple_of((1 - xlo) * T, T), T)], cbuf.at[q], cs.at[q], cr.at[q], partner)
+    for n in range(2):
+        for way in (0, 1):
+            w_arrived(way, 7, 2 * n + way).wait_recv()
+        add(n, (z + 8) % NZ)
+        csrc[n] = acc[n, pl.ds(pl.multiple_of((1 - xlo) * T, T), T), :].astype(jnp.bfloat16)
+        copy = remote(csrc.at[n], cbuf.at[n], cs.at[n], cr.at[n], partner)
         copy.start()
-        sums.append((q, copy))
-    for q, copy in sums:
+        sums.append(copy)
+    for n, copy in enumerate(sums):
         copy.wait_recv()
-        cols = pl.ds(q * LANES, LANES)
-        mixed = acc[q, pl.ds(pl.multiple_of(xlo * T, T), T), :] + cbuf[q]
+        cols = pl.ds(n * WIDE, WIDE)
+        mixed = acc[n, pl.ds(pl.multiple_of(xlo * T, T), T), :] + cbuf[n].astype(F32)
         out[:, cols] = (stream[:, cols].astype(F32) + mixed).astype(jnp.bfloat16)
 
-    for _, copy in sums:
+    for copy in sums:
         copy.wait_send()
     for n, (slot, sem) in enumerate(passed):
         remote(slot, slot, fs.at[n], sem, sibling).wait_send()
@@ -346,7 +348,7 @@
             pltpu.VMEM((POLES, D), F32),
             pltpu.VMEM((POLES, D), F32),
             pltpu.VMEM((T, D), jnp.bfloat16),
-            pltpu.VMEM((Q, NZ, 2 * LANES, LANES), jnp.bfloat16),
+            pltpu.VMEM((2, NZ, WIDE, WIDE), jnp.bfloat16),
             pltpu.VMEM((3, NZ, T, 2 * LANES), jnp.bfloat16),
             pltpu.VMEM((2, T, 2 * LANES), jnp.bfloat16),
             pltpu.VMEM((3, T, D), jnp.bfloat16),
@@ -361,12 +363,13 @@
             pltpu.VMEM((len(ROUNDS), Q, POLES, LANES), F32),
             pltpu.VMEM((7, Q, POLES, LANES), F32),
             pltpu.VMEM((Q, POLES, LANES), F32),
-            pltpu.VMEM((Q, 2 * T, LANES), F32),
-            pltpu.VMEM((Q, T, LANES), F32),
+            pltpu.VMEM((2, 2 * T, WIDE), F32),
+            pltpu.VMEM((2, T, WIDE), jnp.bfloat16),
+            pltpu.VMEM((2, T, WIDE), jnp.bfloat16),
             dma((2, 8, Q)), dma((2, 8, Q)),
             dma((4, 2)), dma((2, 8)), dma((4,)), dma((4,)), dma((8,)),
             dma((7,)), dma((7,)),
-            dma((2,)), dma((Q,)), dma((Q,)), dma((Q + 6,)),
+            dma((2,)), dma((2,)), dma((2,)), dma((Q + 6,)),
         ],
         compiler_params=pltpu.CompilerParams(
             collective_id=0, has_side_effects=True, vmem_limit_bytes=60 * 2**20),

time: 81.3 us -> 77.3 us (0.951)
  Pallas kernels: 79.1 us -> 75.6 us
    pallas_call x1, Pallas kernels: 79.1 us -> 75.6 us  [shards(): pl.pallas_call(kernel, out_shape=jax.ShapeDtypeStruct((T, D), jnp.bfloat1...]
where the time goes in v3:
time: 77.3 us; the launch traced here: 77.2 us
  Pallas kernels  75.6 us (98%)
  local copies, waits for them, and re-layouts  1.57 us (2%)
    pallas_call x1, Pallas kernels, shards(): pl.pallas_call(kernel, out_shape=jax.ShapeDtypeStruct((T, D), jnp.bfloat1...  75.6 us
    unnamed x1, local copies, waits for them, and re-layouts  1.57 us

profile of v3, /device:TPU:4, one launch (start us, length us, event | category | flops | bytes accessed | tf_op | source)
XLA Modules:
  0.0 77.2 jit_solution(1402274388638865607)
XLA Ops:
  0.0 75.6 %shard_map.73 = bf16[128,512]{1,0:T(8,128)(2,1)} custom-call(bf16[3,128,512]{2,1,0:T(8,128)(2,1)} %feat.1, f32[3,3,512]{2,1,0:T(4,128)} %taps_h.1, f32[8,512]{1,0:T(8,128)} %bitcast.3, f32[8,512]{1,0:T(8,128)} %bitcast.4, f32[8,512]{1,0:T(8,128)} %bitcast.5, bf16[128,512]{1,0:T(8,128)(2,1)} %stream_h.1, bf16[256,512]{1,0:T(8,128)(2,1)} %w.1), custom_call_target="tpu_custom_call" | custom-call | tf_op jit(solution)/shard_map/pallas_call | solution.py:340
  75.6 1.6 %copy.9 = bf16[128,512]{1,0:T(8,128)(2,1)} copy(bf16[128,512]{1,0:T(8,128)(2,1)} %shard_map.73) | data formatting | bytes 262144

commit v4 on v3

--- a/solution.py
+++ b/solution.py
@@ -6,10 +6,11 @@
 from jax.sharding import PartitionSpec as P
 
 FIRST, EACH = 3.6, 1.45
-STATE_AT = (10.0, 17.0, 19.5)
-Y_AT = {1: 25.0, 3: 26.0, 2: 28.5}
-X_AT = (29.0, 30.0, 31.0, 33.0, 35.0, 36.0)
-SIBLING_AT = 37.0
+KNOW_AT = (2.5, 5.5, 9.5)
+ENDS_AT, TOTAL_AT, STARTS_AT = 15.0, 18.0, 23.5
+Y_AT = {1: 28.5, 3: 29.5, 2: 31.5}
+X_AT = (32.0, 33.0, 34.0, 36.0, 38.0, 39.0)
+SIBLING_AT = 40.0
 DOT = 0.25
 
 MESH = pl.DeviceIdType.MESH
@@ -23,7 +24,6 @@
 STEPS = T // SUB
 NZ = 16
 NS = 32
-ROUNDS = ((1, 2, 3), (4, 8, 12), (16,))
 
 
 def place():
@@ -33,8 +33,8 @@
 
 
 def kernel(feat, taps_h, dec_h, res_h, sin_h, stream_h, w, out,
-           taps, dec, res, sin, stream, wbuf, gall, gown, fraw, fpad, tail, halo, pbuf, qbuf, ybuf, xs, gf, ibuf, rbuf, sbuf, acc, csrc, cbuf,
-           ws, wr, gs, gr, ys, sr, fs, ks, kr, hs, cs, cr, ls):
+           taps, dec, res, sin, stream, wbuf, gall, gown, fraw, fpad, tail, halo, pbuf, qbuf, ybuf, xs, gf, ends, ends_in, starts, starts_in, dec16, sin16, seed, total_out, total_in, sbuf, acc, csrc, cbuf,
+           ws, wr, gs, gr, ys, sr, fs, es, er, ts, tr, ps, hs, cs, cr, ls, know):
     s, c, xlo, z, y, xhi, core = place()
 
     def dev(xl, zz, yy, xh, co):
@@ -54,20 +54,26 @@
     def greet(to):
         pl.semaphore_signal(barrier, inc=1, device_id=to, device_id_type=MESH)
 
-    hops = (1, 31, 2, 30, 3, 29, 4, 28, 8, 24, 12, 20, 16)
-    for d in hops:
-        greet({"seq": (s + d) % NS, "chan": c})
-    greet(up)
-    greet(down)
-    greet(sibling)
-    mine = xlo * 8 + y * 2 + xhi
-
-    def greet_plane(i, carry):
-        o = (mine + i) % 16
-        greet(dev(o // 8, z, (o // 2) % 4, o % 2, core))
-        return carry
-
-    lax.fori_loop(1, 16, greet_plane, 0)
+    def along_x(dx):
+        x = (xhi * 2 + xlo + dx) % 4
+        return dev(x % 2, z, y, x // 2, core)
+
+    def along_y(dy):
+        return dev(xlo, z, (y + dy) % 4, xhi, core)
+
+    def along_z(dz):
+        return dev(xlo, (z + dz + NZ) % NZ, y, xhi, core)
+
+    near = [up, down, {"seq": (s + 1) % NS, "chan": c}, {"seq": (s + NS - 1) % NS, "chan": c}, sibling,
+            along_x(1), along_x(3), along_y(1), along_y(3)]
+    for to in near:
+        greet(to)
+
+    def tell(n, to):
+        pl.semaphore_signal(know.at[n], inc=1, device_id=to, device_id_type=MESH)
+
+    def heard(n):
+        pl.semaphore_wait(know.at[n], 1)
 
     load_f = pltpu.make_async_copy(feat, fraw, ls.at[Q])
     load_f.start()
@@ -86,7 +92,7 @@
     for o in own_w + small:
         o.wait()
 
-    pl.semaphore_wait(barrier, len(hops) + 3 + 15)
+    pl.semaphore_wait(barrier, len(near))
 
     send_halo = remote(tail, halo, hs.at[0], hs.at[1], {"seq": (s + 1) % NS, "chan": c})
     send_halo.start()
@@ -112,6 +118,11 @@
     for q in range(Q):
         w_send(0, 0, q)
         w_send(1, 0, q)
+
+    tell(0, up)
+    tell(1, down)
+    tell(6, along_y(3))
+    tell(7, along_x(3))
 
     forwards = [(j, q) for j in range(1, 8) for q in range(Q)]
 
@@ -124,6 +135,10 @@
                     w_send(way, j, q)
 
     send_halo.wait_recv()
+    heard(0)
+    heard(1)
+    tell(2, along_z(2))
+    tell(3, along_z(-2))
     first = s > 0
     for i in range(3):
         fpad[i, pl.ds(6, 2), :] = jnp.where(first, halo[pl.ds(2 * i, 2), :], 0.0)
@@ -160,34 +175,83 @@
                 moved = jnp.where(row >= d, pltpu.roll(total, d, 0), 0.0)
                 total = total + jnp.exp(rates[r] * (-1.0 * STEPS * d)) * moved
             xs[q, r] = jnp.where(row >= 1, pltpu.roll(total, 1, 0), 0.0)
-            ibuf[0, q, r:r + 1, :] = total[SUB - 1:SUB, :]
+            ends[q * 4 + r // 2, r % 2:r % 2 + 1, :] = total[SUB - 1:SUB, :]
         return carry
 
     lax.fori_loop(0, Q, inner, 0)
 
-    def decayed(q, blocks):
-        return jnp.exp(dec[:, q * LANES:(q + 1) * LANES] * (-1.0 * T * blocks))
-
     for q in range(Q):
-        sbuf[q] = jnp.exp(dec[:, q * LANES:(q + 1) * LANES] * (-1.0 * T * s.astype(F32))) * sin[:, q * LANES:(q + 1) * LANES]
-    state_sends = []
-    slot = 0
-    for k, distances in enumerate(ROUNDS):
-        copies = [remote(ibuf.at[k], rbuf.at[slot + n], ks.at[slot + n], kr.at[slot + n], {"seq": (s + d) % NS, "chan": c})
-                  for n, d in enumerate(distances)]
-        for copy in copies:
-            copy.start()
-        until(STATE_AT[k])
-        for n, d in enumerate(distances):
-            copies[n].wait_recv()
-            for q in range(Q):
-                got = jnp.where(s >= d, rbuf[slot + n, q], 0.0)
-                sbuf[q] = sbuf[q] + decayed(q, d - 1) * got
-                if k < len(ROUNDS) - 1:
-                    before = ibuf[k, q] if n == 0 else ibuf[k + 1, q]
-                    ibuf[k + 1, q] = before + decayed(q, d) * got
-        slot += len(distances)
-        state_sends += copies
+        for p in range(4):
+            part = (slice(2 * p, 2 * p + 2), slice(q * LANES, (q + 1) * LANES))
+            dec16[q * 4 + p] = dec[part]
+            sin16[q * 4 + p] = sin[part]
+
+    def end_copy(n):
+        to = (z + n) % NZ
+        return remote(ends.at[to], ends_in.at[z], es.at[n], er.at[z], along_z(n))
+
+    def end_arrives(n):
+        came = (z + n) % NZ
+        return remote(ends.at[0], ends_in.at[came], es.at[n], er.at[came], up)
+
+    def start_copy(n):
+        to = (z + n) % NZ
+        return remote(starts.at[to], starts_in.at[z], ts.at[n], tr.at[z], along_z(n))
+
+    def start_arrives(n):
+        came = (z + n) % NZ
+        return remote(starts.at[0], starts_in.at[came], ts.at[n], tr.at[came], up)
+
+    def each(lo, hi, do):
+        def step(n, carry):
+            do(n)
+            return carry
+
+        lax.fori_loop(lo, hi, step, 0)
+
+    until(KNOW_AT[1])
+    heard(2)
+    heard(3)
+    tell(4, along_z(4))
+    tell(5, along_z(-4))
+    each(1, 5, lambda n: end_copy(n).start())
+    each(12, 16, lambda n: end_copy(n).start())
+    ends_in[z] = ends[z]
+    until(KNOW_AT[2])
+    heard(4)
+    heard(5)
+    each(5, 12, lambda n: end_copy(n).start())
+    until(ENDS_AT)
+    each(1, 16, lambda n: end_arrives(n).wait_recv())
+    rate = jnp.exp(dec16[z] * (-1.0 * T))
+    give_total = remote(total_out, total_in, ps.at[0], ps.at[1], partner)
+
+    @pl.when(xlo == 0)
+    def _():
+        seed[...] = sin16[z]
+
+    @pl.when(xlo == 1)
+    def _():
+        give_total.wait_recv()
+        seed[...] = total_in[...]
+
+    state = seed[...]
+    for n in range(NZ):
+        starts[n] = state
+        state = rate * state + ends_in[n]
+
+    @pl.when(xlo == 0)
+    def _():
+        total_out[...] = state
+        give_total.start()
+
+    each(1, 16, lambda n: start_copy(n).start())
+    starts_in[z] = starts[z]
+    until(STARTS_AT)
+    each(1, 16, lambda n: start_arrives(n).wait_recv())
+    for q in range(Q):
+        for p in range(4):
+            sbuf[q, 2 * p:2 * p + 2, :] = starts_in[q * 4 + p]
 
     def gate(q, carry):
         cols = pl.ds(pl.multiple_of(q * LANES, LANES), LANES)
@@ -217,10 +281,6 @@
         k = (yy % 2) * 4 + xhi * 2 + core
         return gall.at[xlo, pl.ds(2 * k, 2)], gr.at[xlo, k]
 
-    def along_x(dx):
-        x = (xhi * 2 + xlo + dx) % 4
-        return dev(x % 2, z, y, x // 2, core)
-
     def send_x(n, src):
         yy = (y + n) % 4
         dst, sem = landing(yy)
@@ -235,6 +295,8 @@
             remote(src, dst, gs.at[n, 0], sem, along_x(1)).start()
             remote(src, dst, gs.at[n, 1], sem, along_x(3)).start()
 
+    heard(6)
+    heard(7)
     home = y // 2 == xlo
 
     @pl.when(home)
@@ -242,7 +304,7 @@
         pltpu.make_async_copy(gown, spot(y), sr.at[y]).start()
 
     send_x(0, gown)
-    y_sends = [remote(gown, spot(y), ys.at[n], sr.at[y], dev(xlo, z, (y + n) % 4, xhi, core)) for n in (1, 2, 3)]
+    y_sends = [remote(gown, spot(y), ys.at[n], sr.at[y], along_y(n)) for n in (1, 2, 3)]
     for copy in y_sends:
         copy.start()
     passed = []
@@ -316,8 +378,13 @@
         copy.wait_send()
     for n, (slot, sem) in enumerate(passed):
         remote(slot, slot, fs.at[n], sem, sibling).wait_send()
-    for copy in state_sends:
-        copy.wait_send()
+    each(1, 16, lambda n: end_copy(n).wait_send())
+    each(1, 16, lambda n: start_copy(n).wait_send())
+
+    @pl.when(xlo == 0)
+    def _():
+        give_total.wait_send()
+
     send_halo.wait_send()
     for way, j, q in sent:
         w_copy(way, j, q).wait_send()
@@ -360,16 +427,17 @@
             pltpu.VMEM((Q, STEPS, SUB, LANES), F32),
             pltpu.VMEM((Q, POLES, SUB, LANES), F32),
             pltpu.VMEM((Q, T, LANES), F32),
-            pltpu.VMEM((len(ROUNDS), Q, POLES, LANES), F32),
-            pltpu.VMEM((7, Q, POLES, LANES), F32),
+            *[pltpu.VMEM((NZ, 2, LANES), F32)] * 6,
+            *[pltpu.VMEM((2, LANES), F32)] * 3,
             pltpu.VMEM((Q, POLES, LANES), F32),
             pltpu.VMEM((2, 2 * T, WIDE), F32),
             pltpu.VMEM((2, T, WIDE), jnp.bfloat16),
             pltpu.VMEM((2, T, WIDE), jnp.bfloat16),
             dma((2, 8, Q)), dma((2, 8, Q)),
             dma((4, 2)), dma((2, 8)), dma((4,)), dma((4,)), dma((8,)),
-            dma((7,)), dma((7,)),
+            dma((NZ,)), dma((NZ,)), dma((NZ,)), dma((NZ,)), dma((2,)),
             dma((2,)), dma((2,)), dma((2,)), dma((Q + 6,)),
+            pltpu.SemaphoreType.REGULAR((8,)),
         ],
         compiler_params=pltpu.CompilerParams(
             collective_id=0, has_side_effects=True, vmem_limit_bytes=60 * 2**20),

time: 77.3 us -> 74.4 us (0.962)
  the two profiles are of different devices: /device:TPU:4 before, /device:TPU:18 now
where the time goes in v4:
time: 74.4 us; the launch traced here: 74.2 us
  Pallas kernels  72.7 us (98%)
  local copies, waits for them, and re-layouts  1.57 us (2%)
    pallas_call x1, Pallas kernels, shards(): pl.pallas_call(kernel, out_shape=jax.ShapeDtypeStruct((T, D), jnp.bfloat1...  72.7 us
    unnamed x1, local copies, waits for them, and re-layouts  1.57 us

profile of v4, /device:TPU:18, one launch (start us, length us, event | category | flops | bytes accessed | tf_op | source)
XLA Modules:
  0.0 74.2 jit_solution(16699222740380435621)
XLA Ops:
  0.0 72.7 %shard_map.73 = bf16[128,512]{1,0:T(8,128)(2,1)} custom-call(bf16[3,128,512]{2,1,0:T(8,128)(2,1)} %feat.1, f32[3,3,512]{2,1,0:T(4,128)} %taps_h.1, f32[8,512]{1,0:T(8,128)} %bitcast.3, f32[8,512]{1,0:T(8,128)} %bitcast.4, f32[8,512]{1,0:T(8,128)} %bitcast.5, bf16[128,512]{1,0:T(8,128)(2,1)} %stream_h.1, bf16[256,512]{1,0:T(8,128)(2,1)} %w.1), custom_call_target="tpu_custom_call" | custom-call | tf_op jit(solution)/shard_map/pallas_call | solution.py:407
  72.7 1.6 %copy.9 = bf16[128,512]{1,0:T(8,128)(2,1)} copy(bf16[128,512]{1,0:T(8,128)(2,1)} %shard_map.73) | data formatting | bytes 262144

commit v5 on v4

--- a/solution.py
+++ b/solution.py
@@ -5,12 +5,12 @@
 from jax.experimental.pallas import tpu as pltpu
 from jax.sharding import PartitionSpec as P
 
-FIRST, EACH = 3.6, 1.45
-KNOW_AT = (2.5, 5.5, 9.5)
-ENDS_AT, TOTAL_AT, STARTS_AT = 15.0, 18.0, 23.5
-Y_AT = {1: 28.5, 3: 29.5, 2: 31.5}
-X_AT = (32.0, 33.0, 34.0, 36.0, 38.0, 39.0)
-SIBLING_AT = 40.0
+FIRST, EACH = 4.2, 1.42
+KNOW_AT = (2.5, 6.0, 11.0)
+ENDS_AT, TOTAL_AT, STARTS_AT = 17.5, 18.0, 26.0
+Y_AT = (30.5, 31.0, 32.0, 32.5, 33.5, 34.5)
+X_AT = (34.5, 34.5, 34.5, 35.5, 35.5, 35.5, 37.0, 37.5, 38.0, 39.0, 40.0, 40.5)
+SIBLING_AT = 41.0
 DOT = 0.25
 
 MESH = pl.DeviceIdType.MESH
@@ -270,43 +270,45 @@
         gown[q // 2, :, pl.ds(pl.multiple_of((q % 2) * LANES, LANES), LANES)] = gf[q].astype(jnp.bfloat16)
         return carry
 
-    lax.fori_loop(0, Q, gate, 0)
-
-    def spot(yy):
+    def spot(yy, h):
         other = (yy // 2 + xlo) % 2
         k = ((yy % 2) * 4 + xhi * 2 + core) * (1 - other) + (yy % 2) * other
-        return gall.at[xlo * (1 - other) + 2 * other, pl.ds(2 * k, 2)]
-
-    def landing(yy):
+        return gall.at[xlo * (1 - other) + 2 * other, 2 * k + h]
+
+    def landing(yy, h):
         k = (yy % 2) * 4 + xhi * 2 + core
-        return gall.at[xlo, pl.ds(2 * k, 2)], gr.at[xlo, k]
-
-    def send_x(n, src):
+        return gall.at[xlo, 2 * k + h], gr.at[xlo, k, h]
+
+    def send_x(n, h, src):
         yy = (y + n) % 4
-        dst, sem = landing(yy)
+        dst, sem = landing(yy, h)
         same = yy // 2 == xlo
 
         @pl.when(same)
         def _():
-            remote(src, dst, gs.at[n, 0], sem, along_x(2)).start()
+            remote(src, dst, gs.at[n, 0, h], sem, along_x(2)).start()
 
         @pl.when(jnp.logical_not(same))
         def _():
-            remote(src, dst, gs.at[n, 0], sem, along_x(1)).start()
-            remote(src, dst, gs.at[n, 1], sem, along_x(3)).start()
+            remote(src, dst, gs.at[n, 0, h], sem, along_x(1)).start()
+            remote(src, dst, gs.at[n, 1, h], sem, along_x(3)).start()
 
     heard(6)
     heard(7)
     home = y // 2 == xlo
-
-    @pl.when(home)
-    def _():
-        pltpu.make_async_copy(gown, spot(y), sr.at[y]).start()
-
-    send_x(0, gown)
-    y_sends = [remote(gown, spot(y), ys.at[n], sr.at[y], along_y(n)) for n in (1, 2, 3)]
-    for copy in y_sends:
-        copy.start()
+    y_sends = []
+    for h in range(2):
+        lax.fori_loop(2 * h, 2 * h + 2, gate, 0)
+
+        @pl.when(home)
+        def _():
+            pltpu.make_async_copy(gown.at[h], spot(y, h), sr.at[y, h]).start()
+
+        send_x(0, h, gown.at[h])
+        for n in (1, 3, 2):
+            copy = remote(gown.at[h], spot(y, h), ys.at[n, h], sr.at[y, h], along_y(n))
+            copy.start()
+            y_sends.append(copy)
     passed = []
 
     def to_sibling(slot, sem):
@@ -314,34 +316,40 @@
         copy.start()
         passed.append((slot, sem))
 
-    for n in (1, 3, 2):
-        until(Y_AT[n])
+    for i, (n, h) in enumerate(((1, 0), (3, 0), (1, 1), (3, 1), (2, 0), (2, 1))):
+        until(Y_AT[i])
         yy = (y + n) % 4
-        remote(spot(yy), spot(yy), ys.at[n], sr.at[yy], sibling).wait_recv()
-        send_x(n, spot(yy))
-
-    def arrived(xl, yy, xh, co):
+        remote(spot(yy, h), spot(yy, h), ys.at[n, h], sr.at[yy, h], sibling).wait_recv()
+        send_x(n, h, spot(yy, h))
+
+    def arrived(xl, yy, xh, co, h):
         k = yy * 4 + xh * 2 + co
-        return gall.at[xl, pl.ds(2 * k, 2)], gr.at[xl, k]
+        return gall.at[xl, 2 * k + h], gr.at[xl, k, h]
 
     @pl.when(home)
     def _():
-        pltpu.make_async_copy(gown, spot(y), sr.at[y]).wait()
+        for h in range(2):
+            pltpu.make_async_copy(gown.at[h], spot(y, h), sr.at[y, h]).wait()
 
     for yy in range(2):
-        to_sibling(*arrived(xlo, yy, xhi, core))
-    for yy in range(2):
-        for xl, xh in ((1 - xlo, xhi), (1 - xlo, 1 - xhi), (xlo, 1 - xhi)):
-            until(X_AT[len(passed) - 2])
-            slot, sem = arrived(xl, yy, xh, core)
-            remote(slot, slot, fs.at[0], sem, sibling).wait_recv()
-            to_sibling(slot, sem)
+        for h in range(2):
+            to_sibling(*arrived(xlo, yy, xhi, core, h))
+    nearer = (y + y // 2 + xlo) % 2
+    for i in range(2):
+        yy = (nearer + i) % 2
+        for h in range(2):
+            for xl, xh in ((1 - xlo, xhi), (1 - xlo, 1 - xhi), (xlo, 1 - xhi)):
+                until(X_AT[len(passed) - 4])
+                slot, sem = arrived(xl, yy, xh, core, h)
+                remote(slot, slot, fs.at[0], sem, sibling).wait_recv()
+                to_sibling(slot, sem)
     until(SIBLING_AT)
     for xl in range(2):
         for yy in range(2):
             for xh in range(2):
-                slot, sem = arrived(xl, yy, xh, 1 - core)
-                remote(slot, slot, fs.at[0], sem, sibling).wait_recv()
+                for h in range(2):
+                    slot, sem = arrived(xl, yy, xh, 1 - core, h)
+                    remote(slot, slot, fs.at[0], sem, sibling).wait_recv()
 
     def add(n, block, fresh=False):
         lhs = gall[pl.ds(0, 2), block].reshape(2 * T, WIDE)
@@ -391,12 +399,13 @@
     for copy in y_sends:
         copy.wait_send()
     for n in range(4):
-        dst, sem = landing((y + n) % 4)
-        remote(gown, dst, gs.at[n, 0], sem, sibling).wait_send()
-
-        @pl.when((y + n) % 4 // 2 != xlo)
-        def _():
-            remote(gown, dst, gs.at[n, 1], sem, sibling).wait_send()
+        for h in range(2):
+            dst, sem = landing((y + n) % 4, h)
+            remote(gown.at[h], dst, gs.at[n, 0, h], sem, sibling).wait_send()
+
+            @pl.when((y + n) % 4 // 2 != xlo)
+            def _():
+                remote(gown.at[h], dst, gs.at[n, 1, h], sem, sibling).wait_send()
 
 
 def shards(stream_in, features, conv_taps, decay, residues, state_in, out_weight):
@@ -434,7 +443,7 @@
             pltpu.VMEM((2, T, WIDE), jnp.bfloat16),
             pltpu.VMEM((2, T, WIDE), jnp.bfloat16),
             dma((2, 8, Q)), dma((2, 8, Q)),
-            dma((4, 2)), dma((2, 8)), dma((4,)), dma((4,)), dma((8,)),
+            dma((4, 2, 2)), dma((2, 8, 2)), dma((4, 2)), dma((4, 2)), dma((16,)),
             dma((NZ,)), dma((NZ,)), dma((NZ,)), dma((NZ,)), dma((2,)),
             dma((2,)), dma((2,)), dma((2,)), dma((Q + 6,)),
             pltpu.SemaphoreType.REGULAR((8,)),

time: 74.4 us -> 69.6 us (0.935)
  the two profiles are of different devices: /device:TPU:18 before, /device:TPU:4 now
where the time goes in v5:
time: 69.6 us; the launch traced here: 69.4 us
  Pallas kernels  67.9 us (98%)
  local copies, waits for them, and re-layouts  1.57 us (2%)
    pallas_call x1, Pallas kernels, shards(): pl.pallas_call(kernel, out_shape=jax.ShapeDtypeStruct((T, D), jnp.bfloat1...  67.9 us
    unnamed x1, local copies, waits for them, and re-layouts  1.57 us

profile of v5, /device:TPU:4, one launch (start us, length us, event | category | flops | bytes accessed | tf_op | source)
XLA Modules:
  0.0 69.4 jit_solution(3808320467841170508)
XLA Ops:
  0.0 67.9 %shard_map.73 = bf16[128,512]{1,0:T(8,128)(2,1)} custom-call(bf16[3,128,512]{2,1,0:T(8,128)(2,1)} %feat.1, f32[3,3,512]{2,1,0:T(4,128)} %taps_h.1, f32[8,512]{1,0:T(8,128)} %bitcast.3, f32[8,512]{1,0:T(8,128)} %bitcast.4, f32[8,512]{1,0:T(8,128)} %bitcast.5, bf16[128,512]{1,0:T(8,128)(2,1)} %stream_h.1, bf16[256,512]{1,0:T(8,128)(2,1)} %w.1), custom_call_target="tpu_custom_call" | custom-call | tf_op jit(solution)/shard_map/pallas_call | solution.py:416
  67.9 1.6 %copy.9 = bf16[128,512]{1,0:T(8,128)(2,1)} copy(bf16[128,512]{1,0:T(8,128)(2,1)} %shard_map.73) | data formatting | bytes 262144

commit v6 on v5

--- a/solution.py
+++ b/solution.py
@@ -6,11 +6,11 @@
 from jax.sharding import PartitionSpec as P
 
 FIRST, EACH = 4.2, 1.42
-KNOW_AT = (2.5, 6.0, 11.0)
-ENDS_AT, TOTAL_AT, STARTS_AT = 17.5, 18.0, 26.0
+KNOW_AT = (2.5, 6.0, 9.5)
+ENDS_AT, STARTS_AT = 17.5, 26.0
 Y_AT = (30.5, 31.0, 32.0, 32.5, 33.5, 34.5)
 X_AT = (34.5, 34.5, 34.5, 35.5, 35.5, 35.5, 37.0, 37.5, 38.0, 39.0, 40.0, 40.5)
-SIBLING_AT = 41.0
+SIBLING_AT = 44.0
 DOT = 0.25
 
 MESH = pl.DeviceIdType.MESH
@@ -84,18 +84,21 @@
         ((taps_h, taps), (dec_h, dec), (res_h, res), (sin_h, sin), (stream_h, stream)))]
     for o in small:
         o.start()
+
     load_f.wait()
     for i in range(3):
         fpad[i, pl.ds(8, T), :] = fraw[i].astype(F32)
         tail[pl.ds(2 * i, 2), :] = fpad[i, pl.ds(8 + T - 2, 2), :]
     tail[pl.ds(6, 2), :] = jnp.zeros((2, Q * LANES), F32)
-    for o in own_w + small:
+    for o in own_w:
         o.wait()
-
     pl.semaphore_wait(barrier, len(near))
-
     send_halo = remote(tail, halo, hs.at[0], hs.at[1], {"seq": (s + 1) % NS, "chan": c})
     send_halo.start()
+    tell(0, up)
+    tell(1, down)
+    tell(6, along_y(3))
+    tell(7, along_x(3))
 
     def chunk(block, q):
         return wbuf.at[q // 2, block, pl.ds(q % 2 * LANES, LANES)]
@@ -119,10 +122,6 @@
         w_send(0, 0, q)
         w_send(1, 0, q)
 
-    tell(0, up)
-    tell(1, down)
-    tell(6, along_y(3))
-    tell(7, along_x(3))
 
     forwards = [(j, q) for j in range(1, 8) for q in range(Q)]
 
@@ -133,6 +132,9 @@
                 w_arrived(way, j - 1, q).wait_recv()
                 if j < 7 or q % 2 == way:
                     w_send(way, j, q)
+
+    for o in small:
+        o.wait()
 
     send_halo.wait_recv()
     heard(0)
@@ -209,13 +211,13 @@
 
         lax.fori_loop(lo, hi, step, 0)
 
-    until(KNOW_AT[1])
     heard(2)
     heard(3)
     tell(4, along_z(4))
     tell(5, along_z(-4))
     each(1, 5, lambda n: end_copy(n).start())
     each(12, 16, lambda n: end_copy(n).start())
+    until(KNOW_AT[1])
     ends_in[z] = ends[z]
     until(KNOW_AT[2])
     heard(4)
@@ -304,11 +306,11 @@
         def _():
             pltpu.make_async_copy(gown.at[h], spot(y, h), sr.at[y, h]).start()
 
-        send_x(0, h, gown.at[h])
         for n in (1, 3, 2):
             copy = remote(gown.at[h], spot(y, h), ys.at[n, h], sr.at[y, h], along_y(n))
             copy.start()
             y_sends.append(copy)
+        send_x(0, h, gown.at[h])
     passed = []
 
     def to_sibling(slot, sem):
@@ -367,6 +369,30 @@
                 until(FIRST + EACH * (4 * (forwards[0][0] - 1) + forwards[0][1]))
             for n in range(2):
                 add(n, block)
+    for n, (slot, sem) in enumerate(passed):
+        remote(slot, slot, fs.at[n], sem, sibling).wait_send()
+    each(1, 16, lambda n: end_copy(n).wait_send())
+    each(1, 16, lambda n: start_copy(n).wait_send())
+
+    @pl.when(xlo == 0)
+    def _():
+        give_total.wait_send()
+
+    send_halo.wait_send()
+    for way, j, q in sent:
+        if j < 7:
+            w_copy(way, j, q).wait_send()
+    for copy in y_sends:
+        copy.wait_send()
+    for n in range(4):
+        for h in range(2):
+            dst, sem = landing((y + n) % 4, h)
+            remote(gown.at[h], dst, gs.at[n, 0, h], sem, sibling).wait_send()
+
+            @pl.when((y + n) % 4 // 2 != xlo)
+            def _():
+                remote(gown.at[h], dst, gs.at[n, 1, h], sem, sibling).wait_send()
+
     sums = []
     for n in range(2):
         for way in (0, 1):
@@ -384,28 +410,9 @@
 
     for copy in sums:
         copy.wait_send()
-    for n, (slot, sem) in enumerate(passed):
-        remote(slot, slot, fs.at[n], sem, sibling).wait_send()
-    each(1, 16, lambda n: end_copy(n).wait_send())
-    each(1, 16, lambda n: start_copy(n).wait_send())
-
-    @pl.when(xlo == 0)
-    def _():
-        give_total.wait_send()
-
-    send_halo.wait_send()
     for way, j, q in sent:
-        w_copy(way, j, q).wait_send()
-    for copy in y_sends:
-        copy.wait_send()
-    for n in range(4):
-        for h in range(2):
-            dst, sem = landing((y + n) % 4, h)
-            remote(gown.at[h], dst, gs.at[n, 0, h], sem, sibling).wait_send()
-
-            @pl.when((y + n) % 4 // 2 != xlo)
-            def _():
-                remote(gown.at[h], dst, gs.at[n, 1, h], sem, sibling).wait_send()
+        if j == 7:
+            w_copy(way, j, q).wait_send()
 
 
 def shards(stream_in, features, conv_taps, decay, residues, state_in, out_weight):

time: 69.6 us -> 69 us (level)
  Pallas kernels: 67.9 us -> 67.2 us
where the time goes in v6:
time: 69 us; the launch traced here: 68.8 us
  Pallas kernels  67.2 us (97%)
  local copies, waits for them, and re-layouts  1.57 us (2%)
    pallas_call x1, Pallas kernels, shards(): pl.pallas_call(kernel, out_shape=jax.ShapeDtypeStruct((T, D), jnp.bfloat1...  67.2 us
    unnamed x1, local copies, waits for them, and re-layouts  1.57 us

profile of v6, /device:TPU:4, one launch (start us, length us, event | category | flops | bytes accessed | tf_op | source)
XLA Modules:
  0.0 68.8 jit_solution(16722426385527955105)
XLA Ops:
  0.0 67.2 %shard_map.73 = bf16[128,512]{1,0:T(8,128)(2,1)} custom-call(bf16[3,128,512]{2,1,0:T(8,128)(2,1)} %feat.1, f32[3,3,512]{2,1,0:T(4,128)} %taps_h.1, f32[8,512]{1,0:T(8,128)} %bitcast.3, f32[8,512]{1,0:T(8,128)} %bitcast.4, f32[8,512]{1,0:T(8,128)} %bitcast.5, bf16[128,512]{1,0:T(8,128)(2,1)} %stream_h.1, bf16[256,512]{1,0:T(8,128)(2,1)} %w.1), custom_call_target="tpu_custom_call" | custom-call | tf_op jit(solution)/shard_map/pallas_call | solution.py:423
  67.2 1.6 %copy.9 = bf16[128,512]{1,0:T(8,128)(2,1)} copy(bf16[128,512]{1,0:T(8,128)(2,1)} %shard_map.73) | data formatting | bytes 262144

commit v7 on v6

--- a/solution.py
+++ b/solution.py
@@ -154,7 +154,13 @@
             return total + taps[i, 2:3, cols] * fpad[i, pl.ds(6, T), cols]
 
         pbuf[q] = short(1) * short(2)
-        qbuf[q] = short(0)
+        return carry
+
+    def conv_q(q, carry):
+        cols = pl.ds(pl.multiple_of(q * LANES, LANES), LANES)
+        total = taps[0, 0:1, cols] * fpad[0, pl.ds(8, T), cols]
+        total = total + taps[0, 1:2, cols] * fpad[0, pl.ds(7, T), cols]
+        qbuf[q] = total + taps[0, 2:3, cols] * fpad[0, pl.ds(6, T), cols]
         return carry
 
     lax.fori_loop(0, Q, conv, 0)
@@ -223,6 +229,7 @@
     heard(4)
     heard(5)
     each(5, 12, lambda n: end_copy(n).start())
+    lax.fori_loop(0, Q, conv_q, 0)
     until(ENDS_AT)
     each(1, 16, lambda n: end_arrives(n).wait_recv())
     rate = jnp.exp(dec16[z] * (-1.0 * T))
@@ -397,16 +404,20 @@
     for n in range(2):
         for way in (0, 1):
             w_arrived(way, 7, 2 * n + way).wait_recv()
-        add(n, (z + 8) % NZ)
-        csrc[n] = acc[n, pl.ds(pl.multiple_of((1 - xlo) * T, T), T), :].astype(jnp.bfloat16)
+        far = (z + 8) % NZ
+        theirs = pl.ds(pl.multiple_of((1 - xlo) * T, T), T)
+        last = jnp.dot(gall[1 - xlo, far], wbuf[n, far], preferred_element_type=F32)
+        csrc[n] = (acc[n, theirs, :] + last).astype(jnp.bfloat16)
         copy = remote(csrc.at[n], cbuf.at[n], cs.at[n], cr.at[n], partner)
         copy.start()
         sums.append(copy)
     for n, copy in enumerate(sums):
+        cols = pl.ds(n * WIDE, WIDE)
+        far = (z + 8) % NZ
+        mixed = acc[n, pl.ds(pl.multiple_of(xlo * T, T), T), :] + stream[:, cols].astype(F32)
+        mixed = mixed + jnp.dot(gall[xlo, far], wbuf[n, far], preferred_element_type=F32)
         copy.wait_recv()
-        cols = pl.ds(n * WIDE, WIDE)
-        mixed = acc[n, pl.ds(pl.multiple_of(xlo * T, T), T), :] + cbuf[n].astype(F32)
-        out[:, cols] = (stream[:, cols].astype(F32) + mixed).astype(jnp.bfloat16)
+        out[:, cols] = (mixed + cbuf[n].astype(F32)).astype(jnp.bfloat16)
 
     for copy in sums:
         copy.wait_send()

time: 69 us -> 68.9 us (level)
  no operation moved by 1% of the time
where the time goes in v7:
time: 68.9 us; the launch traced here: 68.8 us
  Pallas kernels  67.2 us (98%)
  local copies, waits for them, and re-layouts  1.57 us (2%)
    pallas_call x1, Pallas kernels, shards(): pl.pallas_call(kernel, out_shape=jax.ShapeDtypeStruct((T, D), jnp.bfloat1...  67.2 us
    unnamed x1, local copies, waits for them, and re-layouts  1.57 us

profile of v7, /device:TPU:4, one launch (start us, length us, event | category | flops | bytes accessed | tf_op | source)
XLA Modules:
  0.0 68.8 jit_solution(15893834367335494561)
XLA Ops:
  0.0 67.2 %shard_map.73 = bf16[128,512]{1,0:T(8,128)(2,1)} custom-call(bf16[3,128,512]{2,1,0:T(8,128)(2,1)} %feat.1, f32[3,3,512]{2,1,0:T(4,128)} %taps_h.1, f32[8,512]{1,0:T(8,128)} %bitcast.3, f32[8,512]{1,0:T(8,128)} %bitcast.4, f32[8,512]{1,0:T(8,128)} %bitcast.5, bf16[128,512]{1,0:T(8,128)(2,1)} %stream_h.1, bf16[256,512]{1,0:T(8,128)(2,1)} %w.1), custom_call_target="tpu_custom_call" | custom-call | tf_op jit(solution)/shard_map/pallas_call | solution.py:434
  67.2 1.6 %copy.9 = bf16[128,512]{1,0:T(8,128)(2,1)} copy(bf16[128,512]{1,0:T(8,128)(2,1)} %shard_map.73) | data formatting | bytes 262144
